TPU v7x, 256 devices: a whole 4x4x8 slice. The times are simulated.
256 devices in a mesh: adapter: 64 (over z, y, core), tensor: 4 (over x).
Axes of the slice: x: 4, y: 4, z: 8, core: 2. Of those that a mesh axis runs over, the one named last changes fastest.
Arguments:
- inputs: bfloat16 [32768, 5120], P('adapter', 'tensor'), may hold values from -6 to 6
- grad_key: bfloat16 [32768, 1024], P('adapter', 'tensor'), may hold values from -6 to 6
- grad_value: bfloat16 [32768, 1024], P('adapter', 'tensor'), may hold values from -6 to 6
- weight_key: bfloat16 [5120, 1024], P(None, 'tensor'), may hold values from -0.1875 to 0.1875
- weight_value: bfloat16 [5120, 1024], P(None, 'tensor'), may hold values from -0.1875 to 0.1875
- down_key: bfloat16 [1024, 16, 5120], P('adapter', None, 'tensor'), may hold values from -0.078125 to 0.078125
- down_value: bfloat16 [1024, 16, 5120], P('adapter', None, 'tensor'), may hold values from -0.078125 to 0.078125
- up_key: bfloat16 [1024, 16, 1024], P('adapter', None, 'tensor'), may hold values from -0.1875 to 0.1875
- up_value: bfloat16 [1024, 16, 1024], P('adapter', None, 'tensor'), may hold values from -0.1875 to 0.1875
- adapter_ids: int32 [32768], P('adapter'), may hold values from 0 to 1023, as said below
Outputs:
- input_gradient: bfloat16 [32768, 5120], P('adapter', 'tensor')
- grad_down_key: float32 [1024, 16, 5120], P('adapter', None, 'tensor')
- grad_down_value: float32 [1024, 16, 5120], P('adapter', None, 'tensor')
- up_key_gradient: float32 [1024, 16, 1024], P('adapter', None, 'tensor')
- up_value_gradient: float32 [1024, 16, 1024], P('adapter', None, 'tensor')
Inputs may be any that keep to these rules, and one draw needn't show every extreme that they name: In each aligned block of 512 tokens (those of one index of adapter), at most 16 tokens have adapters of one owner (adapter_ids // 16), and in every block exactly 16 tokens have adapters of one owner that is the same for all blocks.
All inputs are finite; a program needn't handle non-finite values.
Results may differ from a plain program's by a relative error of at most 0.0034.
Values may be sent and summed in bfloat16 or wider, within the bound.
No kernel may reach another device: no remote copies, remote signals or barrier semaphores. Data moves between devices by JAX's collectives and lax.ppermute only.
A program may use at most 128 MiB of HBM per device.

v0:
```python
import jax
import jax.numpy as jnp
from jax import lax
from jax.sharding import PartitionSpec as P

adapter_scale = 2.0


def project_rows(rows, weights, hot_rows):
    expanded = lax.dot_general(
        rows, weights, (((1,), (2,)), ((), ())), preferred_element_type=jnp.float32
    )
    return jnp.einsum("mlr,ml->rm", expanded, hot_rows.astype(jnp.float32))


def spread_rows(values, hot_rows):
    adapter_rank_count = values.shape[0]
    spread = hot_rows[:, :, None] * values.T[:, None, :]
    return spread.reshape(hot_rows.shape[0], hot_rows.shape[1] * adapter_rank_count)


def contract_token_rows(left, right):
    return lax.dot_general(
        left, right, (((0,), (0,)), ((), ())), preferred_element_type=jnp.float32
    )


def local(
    inputs,
    grad_key,
    grad_value,
    weight_key,
    weight_value,
    down_key,
    down_value,
    up_key,
    up_value,
    adapter_ids,
):
    groups = lax.axis_size("adapter")
    tok_rows = inputs.shape[0]
    local_count = down_key.shape[0]
    adapter_rank_count = down_key.shape[1]
    width_part = down_key.shape[2]
    kv_part = up_key.shape[2]
    capacity = max(2, 2 * tok_rows // groups)
    owner_ids = adapter_ids // local_count
    within = adapter_ids % local_count
    owner_hot = (owner_ids[:, None] == jnp.arange(groups, dtype=jnp.int32)[None, :]).astype(
        jnp.float32
    )
    earlier = (jnp.arange(tok_rows)[:, None] > jnp.arange(tok_rows)[None, :]).astype(jnp.float32)
    before = jnp.dot(earlier, owner_hot, precision=lax.Precision.HIGHEST)
    slot_index = jnp.sum(before * owner_hot, axis=1).astype(jnp.int32)
    target = owner_ids * capacity + slot_index
    route_tokens = (
        jnp.arange(groups * capacity, dtype=jnp.int32)[:, None] == target[None, :]
    ).astype(jnp.bfloat16)
    local_hot = (within[:, None] == jnp.arange(local_count, dtype=jnp.int32)[None, :]).astype(
        jnp.bfloat16
    )

    def place_rows(values):
        return jnp.dot(route_tokens, values, preferred_element_type=jnp.float32).astype(
            jnp.bfloat16
        )

    input_rows, key_row_block, value_row_block, hot_rows = (
        lax.all_to_all(place_rows(inputs), "adapter", split_axis=0, concat_axis=0, tiled=True),
        lax.all_to_all(place_rows(grad_key), "adapter", split_axis=0, concat_axis=0, tiled=True),
        lax.all_to_all(place_rows(grad_value), "adapter", split_axis=0, concat_axis=0, tiled=True),
        lax.all_to_all(place_rows(local_hot), "adapter", split_axis=0, concat_axis=0, tiled=True),
    )
    stacked = jnp.concatenate(
        [
            project_rows(input_rows, down_key, hot_rows),
            project_rows(input_rows, down_value, hot_rows),
            project_rows(key_row_block, up_key, hot_rows),
            project_rows(value_row_block, up_value, hot_rows),
        ],
        axis=0,
    )
    summed_gradient = lax.psum(stacked, "tensor")
    reduced_key = summed_gradient[:adapter_rank_count].astype(jnp.bfloat16)
    reduced_value = summed_gradient[adapter_rank_count : 2 * adapter_rank_count].astype(
        jnp.bfloat16
    )
    backward_key = (
        adapter_scale * summed_gradient[2 * adapter_rank_count : 3 * adapter_rank_count]
    ).astype(jnp.bfloat16)
    backward_value = (adapter_scale * summed_gradient[3 * adapter_rank_count :]).astype(
        jnp.bfloat16
    )
    spread_back_key = spread_rows(backward_key, hot_rows)
    spread_back_value = spread_rows(backward_value, hot_rows)
    spread_reduced_key = spread_rows(reduced_key, hot_rows)
    spread_reduced_value = spread_rows(reduced_value, hot_rows)
    grad_down_key = contract_token_rows(spread_back_key, input_rows).reshape(
        local_count, adapter_rank_count, width_part
    )
    grad_down_value = contract_token_rows(spread_back_value, input_rows).reshape(
        local_count, adapter_rank_count, width_part
    )
    up_key_gradient = (
        adapter_scale * contract_token_rows(spread_reduced_key, key_row_block)
    ).reshape(local_count, adapter_rank_count, kv_part)
    up_value_gradient = (
        adapter_scale * contract_token_rows(spread_reduced_value, value_row_block)
    ).reshape(local_count, adapter_rank_count, kv_part)
    joined_backward = jnp.concatenate([spread_back_key, spread_back_value], axis=1)
    joined_down_weight = jnp.concatenate(
        [
            down_key.reshape(local_count * adapter_rank_count, width_part),
            down_value.reshape(local_count * adapter_rank_count, width_part),
        ],
        axis=0,
    )
    adapter_rows = jnp.dot(
        joined_backward, joined_down_weight, preferred_element_type=jnp.float32
    ).astype(jnp.bfloat16)
    returned_gradients = lax.all_to_all(
        adapter_rows, "adapter", split_axis=0, concat_axis=0, tiled=True
    )
    adapter_input_gradient = contract_token_rows(route_tokens, returned_gradients)
    partial_grad = lax.dot_general(
        grad_key, weight_key, (((1,), (1,)), ((), ())), preferred_element_type=jnp.float32
    )
    partial_grad = partial_grad + lax.dot_general(
        grad_value, weight_value, (((1,), (1,)), ((), ())), preferred_element_type=jnp.float32
    )
    frozen_input_gradient = lax.psum_scatter(
        partial_grad, "tensor", scatter_dimension=1, tiled=True
    )
    input_gradient = (frozen_input_gradient + adapter_input_gradient).astype(jnp.bfloat16)
    return (input_gradient, grad_down_key, grad_down_value, up_key_gradient, up_value_gradient)


def solution(mesh):
    placed = (
        P("adapter", "tensor"),
        P("adapter", "tensor"),
        P("adapter", "tensor"),
        P(None, "tensor"),
        P(None, "tensor"),
        P("adapter", None, "tensor"),
        P("adapter", None, "tensor"),
        P("adapter", None, "tensor"),
        P("adapter", None, "tensor"),
        P("adapter"),
    )
    return jax.shard_map(
        local,
        mesh=mesh,
        in_specs=placed,
        out_specs=(
            P("adapter", "tensor"),
            P("adapter", None, "tensor"),
            P("adapter", None, "tensor"),
            P("adapter", None, "tensor"),
            P("adapter", None, "tensor"),
        ),
        check_vma=False,
    )
```

profile of v0, /device:TPU:8, one launch (start us, length us, event | category | flops | bytes accessed | tf_op | source)
XLA Modules:
  0.0 310.7 jit_solution(16880267166570992710)
XLA Ops:
  7.2 0.0 copy-start
  7.2 0.9 add_select_fusion
  8.0 0.3 fusion.13
  8.3 0.5 fusion.14
  8.8 0.2 all_to_all.38
  9.1 0.2 copy.36
  9.3 0.8 reshape.94
  10.1 12.1 %all-to-all-start = ((bf16[64,2,128]{2,1,0:T(2,128)(2,1)}), bf16[64,2,128]{2,1,0:T(2,128)(2,1)S(1)}, u32[]{:S(2)}, u32[]{:S(2)}) async-start(bf16[64,2,128]{2,1,0:T(2,128)(2,1)} %reshape.94), calls=%async_computation.1 | async-start | bytes 65536 | tf_op jit(solution)/shard_map/all_to_all | solution.py:72
  22.2 2.2 fusion.8
  24.4 6.3 %all-to-all-done = bf16[64,2,128]{2,1,0:T(2,128)(2,1)S(1)} async-done(((bf16[64,2,128]{2,1,0:T(2,128)(2,1)}), bf16[64,2,128]{2,1,0:T(2,128)(2,1)S(1)}, u32[]{:S(2)}, u32[]{:S(2)}) %all-to-all-start) | async-done | bytes 32800 | tf_op jit(solution)/shard_map/all_to_all | solution.py:72
  30.7 5.5 %all-to-all-start.3 = ((bf16[64,16,256]{2,1,0:T(8,128)(2,1)}), bf16[64,16,256]{2,1,0:T(8,128)(2,1)S(1)}, u32[]{:S(2)}, u32[]{:S(2)}) async-start(bf16[64,16,256]{2,1,0:T(8,128)(2,1)} %bitcast.86), calls=%async_computation.4 | async-start | bytes 1048576 | tf_op jit(solution)/shard_map/all_to_all | solution.py:71
  36.2 1.3 fusion.7
  37.5 16.4 %all-to-all-done.3 = bf16[64,16,256]{2,1,0:T(8,128)(2,1)S(1)} async-done(((bf16[64,16,256]{2,1,0:T(8,128)(2,1)}), bf16[64,16,256]{2,1,0:T(8,128)(2,1)S(1)}, u32[]{:S(2)}, u32[]{:S(2)}) %all-to-all-start.3) | async-done | bytes 524320 | tf_op jit(solution)/shard_map/all_to_all | solution.py:71
  53.9 6.1 %all-to-all-start.2 = ((bf16[64,16,256]{2,1,0:T(8,128)(2,1)}), bf16[64,16,256]{2,1,0:T(8,128)(2,1)}, u32[]{:S(2)}, u32[]{:S(2)}) async-start(bf16[64,16,256]{2,1,0:T(8,128)(2,1)} %bitcast.87), calls=%async_computation.3 | async-start | bytes 1048576 | tf_op jit(solution)/shard_map/all_to_all | solution.py:70
  60.0 4.4 %convolution_convert_fusion = bf16[1024,1280]{1,0:T(8,128)(2,1)} fusion(bf16[512,1280]{1,0:T(8,128)(2,1)} %param.10, s32[512]{0:T(512)S(1)} %convert_add_fusion), kind=kOutput, calls=%fused_computation.1 | convolution fusion | flops 1344012288 | bytes 3934208 | tf_op jit(solution)/shard_map/dot_general | solution.py:64
  64.3 13.1 %all-to-all-done.2 = bf16[64,16,256]{2,1,0:T(8,128)(2,1)} async-done(((bf16[64,16,256]{2,1,0:T(8,128)(2,1)}), bf16[64,16,256]{2,1,0:T(8,128)(2,1)}, u32[]{:S(2)}, u32[]{:S(2)}) %all-to-all-start.2) | async-done | bytes 524320 | tf_op jit(solution)/shard_map/all_to_all | solution.py:70
  77.4 6.0 %all-to-all-start.1 = ((bf16[64,16,1280]{2,1,0:T(8,128)(2,1)}), bf16[64,16,1280]{2,1,0:T(8,128)(2,1)}, u32[]{:S(2)}, u32[]{:S(2)}) async-start(bf16[64,16,1280]{2,1,0:T(8,128)(2,1)} %bitcast.76), calls=%async_computation.2 | async-start | bytes 5242880 | tf_op jit(solution)/shard_map/all_to_all | solution.py:69
  83.5 0.0 all-reduce.2.cloned.1.call-start
  83.6 5.5 %fusion.35 = f32[512,5120]{1,0:T(8,128)} fusion(bf16[512,256]{1,0:T(8,128)(2,1)S(1)} %copy-done.3, bf16[5120,256]{1,0:T(8,128)(2,1)S(1)} %copy-done), kind=kOutput, calls=%fused_computation.68 | convolution fusion | flops 1342177280 | bytes 13369344 | tf_op jit(solution)/shard_map/dot_general | solution.py:125
  89.1 0.2 reshape.95
  89.3 0.8 copy.16
  90.1 1.3 mul.97
  91.4 0.0 copy-done.1
  91.4 1.2 fusion.12
  92.6 1.4 fusion.11
  94.0 51.9 %all-to-all-done.1 = bf16[64,16,1280]{2,1,0:T(8,128)(2,1)} async-done(((bf16[64,16,1280]{2,1,0:T(8,128)(2,1)}), bf16[64,16,1280]{2,1,0:T(8,128)(2,1)}, u32[]{:S(2)}, u32[]{:S(2)}) %all-to-all-start.1) | async-done | bytes 2621472 | tf_op jit(solution)/shard_map/all_to_all | solution.py:69
  145.9 2.8 fusion.10
  148.8 0.0 copy-start.2
  148.8 2.7 fusion.9
  151.5 0.7 pad_maximum_fusion
  152.2 0.0 all-reduce.2.cloned.1.call-update
  152.2 0.2 reduce-scatter.2.cloned.1.call-start
  152.4 0.0 copy-done.2
  152.4 10.3 %convolution_add_fusion = f32[512,5120]{1,0:T(8,128)} fusion(f32[512,5120]{1,0:T(8,128)} %fusion.35, bf16[512,256]{1,0:T(8,128)(2,1)S(1)} %copy-done.2, bf16[5120,256]{1,0:T(8,128)(2,1)} %param.14), kind=kOutput, calls=%fused_computation | convolution fusion | flops 1344798720 | bytes 23855104 | tf_op jit(solution)/shard_map/dot_general | solution.py:128
  162.8 0.0 reduce-scatter.2.cloned.1.call-update
  162.8 32.5 %all-reduce.2.cloned.1.call-done = f32[64,1024]{1,0:T(8,128)} async-done(((f32[64,1024]{1,0:T(8,128)}), f32[64,1024]{1,0:T(8,128)}) %all-reduce.2.cloned.1.call-update) | async-done | bytes 262160 | tf_op jit(solution)/shard_map/psum | solution.py:83
  195.3 1.1 convert.4
  196.4 0.9 fusion.31
  197.3 0.9 broadcast_multiply_fusion
  198.2 3.0 convolution_convert_fusion.1
  201.3 10.7 %all-to-all-start.4 = ((bf16[64,16,1280]{2,1,0:T(8,128)(2,1)}), bf16[64,16,1280]{2,1,0:T(8,128)(2,1)}, u32[]{:S(2)}, u32[]{:S(2)}) async-start(bf16[64,16,1280]{2,1,0:T(8,128)(2,1)} %bitcast.77), calls=%async_computation.5 | async-start | bytes 5242880 | tf_op jit(solution)/shard_map/all_to_all | solution.py:121
  212.0 2.2 convolution_multiply_fusion.5
  214.2 2.0 convolution_multiply_fusion.4
  216.3 3.6 %fusion.25 = f32[16,16,1280]{2,1,0:T(8,128)} fusion(bf16[1024,1280,1]{1,0,2:T(8,128)(2,1)} %bitcast.2, bf16[1024,16]{0,1:T(8,128)(2,1)S(1)} %get-tuple-element.5, bf16[1024,16]{0,1:T(8,128)(2,1)S(1)} %mul.97), kind=kOutput, calls=%fused_computation.38 | convolution fusion | flops 671350784 | bytes 3997696 | tf_op jit(solution)/shard_map/dot_general | solution.py:23
  219.9 3.6 %fusion.23 = f32[16,16,1280]{2,1,0:T(8,128)} fusion(bf16[1024,1280,1]{1,0,2:T(8,128)(2,1)} %bitcast.2, bf16[1024,16]{0,1:T(8,128)(2,1)S(1)} %get-tuple-element.6, bf16[1024,16]{0,1:T(8,128)(2,1)S(1)} %mul.97), kind=kOutput, calls=%fused_computation.36 | convolution fusion | flops 671350784 | bytes 3997696 | tf_op jit(solution)/shard_map/dot_general | solution.py:23
  223.6 50.9 %all-to-all-done.4 = bf16[64,16,1280]{2,1,0:T(8,128)(2,1)} async-done(((bf16[64,16,1280]{2,1,0:T(8,128)(2,1)}), bf16[64,16,1280]{2,1,0:T(8,128)(2,1)}, u32[]{:S(2)}, u32[]{:S(2)}) %all-to-all-start.4) | async-done | bytes 2621472 | tf_op jit(solution)/shard_map/all_to_all | solution.py:121
  274.5 24.2 %reduce-scatter.2.cloned.1.call-done = f32[512,1280]{1,0:T(8,128)} async-done(((f32[512,5120]{1,0:T(8,128)}), f32[512,1280]{1,0:T(8,128)}) %reduce-scatter.2.cloned.1.call-update) | async-done | bytes 2621456 | tf_op jit(solution)/shard_map/reduce_scatter | solution.py:131
  298.7 5.2 %fusion = bf16[512,1280]{1,0:T(8,128)(2,1)} fusion(f32[512,1280]{1,0:T(8,128)} %reduce-scatter.2.cloned.1.call-done, bf16[1024,1280]{1,0:T(8,128)(2,1)} %bitcast.21, s32[512]{0:T(512)S(1)} %convert_add_fusion), kind=kOutput, calls=%fused_computation.4 | convolution fusion | flops 1344012288 | bytes 6555648 | tf_op jit(solution)/shard_map/dot_general | solution.py:23
  (13 shorter events, 0.0 us)
Async XLA Ops:
  7.2 76.4 %copy-start = (bf16[5120,256]{1,0:T(8,128)(2,1)S(1)}, bf16[5120,256]{1,0:T(8,128)(2,1)}, u32[]{:S(2)}) copy-start(bf16[5120,256]{1,0:T(8,128)(2,1)} %param.13) | copy-start | bytes 7864324
  7.2 29.0 %copy-start.3 = (bf16[512,256]{1,0:T(8,128)(2,1)S(1)}, bf16[512,256]{1,0:T(8,128)(2,1)}, u32[]{:S(2)}) copy-start(bf16[512,256]{1,0:T(8,128)(2,1)} %param.11) | copy-start | bytes 786436
  10.1 20.6 %all-to-all-start = ((bf16[64,2,128]{2,1,0:T(2,128)(2,1)}), bf16[64,2,128]{2,1,0:T(2,128)(2,1)S(1)}, u32[]{:S(2)}, u32[]{:S(2)}) async-start(bf16[64,2,128]{2,1,0:T(2,128)(2,1)} %reshape.94), calls=%async_computation.1 | async-start | bytes 65536 | tf_op jit(solution)/shard_map/all_to_all | solution.py:72
  30.7 23.2 %all-to-all-start.3 = ((bf16[64,16,256]{2,1,0:T(8,128)(2,1)}), bf16[64,16,256]{2,1,0:T(8,128)(2,1)S(1)}, u32[]{:S(2)}, u32[]{:S(2)}) async-start(bf16[64,16,256]{2,1,0:T(8,128)(2,1)} %bitcast.86), calls=%async_computation.4 | async-start | bytes 1048576 | tf_op jit(solution)/shard_map/all_to_all | solution.py:71
  53.9 37.5 %copy-start.1 = (bf16[64,16,256]{2,1,0:T(8,128)(2,1)}, bf16[64,16,256]{2,1,0:T(8,128)(2,1)S(1)}, u32[]{:S(2)}) copy-start(bf16[64,16,256]{2,1,0:T(8,128)(2,1)S(1)} %all-to-all-done.3) | copy-start | bytes 1572868
  53.9 23.6 %all-to-all-start.2 = ((bf16[64,16,256]{2,1,0:T(8,128)(2,1)}), bf16[64,16,256]{2,1,0:T(8,128)(2,1)}, u32[]{:S(2)}, u32[]{:S(2)}) async-start(bf16[64,16,256]{2,1,0:T(8,128)(2,1)} %bitcast.87), calls=%async_computation.3 | async-start | bytes 1048576 | tf_op jit(solution)/shard_map/all_to_all | solution.py:70
  77.4 68.5 %all-to-all-start.1 = ((bf16[64,16,1280]{2,1,0:T(8,128)(2,1)}), bf16[64,16,1280]{2,1,0:T(8,128)(2,1)}, u32[]{:S(2)}, u32[]{:S(2)}) async-start(bf16[64,16,1280]{2,1,0:T(8,128)(2,1)} %bitcast.76), calls=%async_computation.2 | async-start | bytes 5242880 | tf_op jit(solution)/shard_map/all_to_all | solution.py:69
  83.5 111.8 %all-reduce.2.cloned.1.call-start = ((), (), s32[]{:S(2)}) async-start(), calls=%async_computation.7 | async-start | bytes 524288 | tf_op jit(solution)/shard_map/psum | solution.py:83
  145.9 2.8 copy-start.5
  148.8 3.7 %copy-start.2 = (bf16[512,256]{1,0:T(8,128)(2,1)S(1)}, bf16[512,256]{1,0:T(8,128)(2,1)}, u32[]{:S(2)}) copy-start(bf16[512,256]{1,0:T(8,128)(2,1)} %param.12) | copy-start | bytes 786436
  152.2 146.5 %reduce-scatter.2.cloned.1.call-start = ((), (), s32[]{:S(2)}) async-start(), calls=%async_computation.6 | async-start | bytes 13107200 | tf_op jit(solution)/shard_map/reduce_scatter | solution.py:131
  195.3 2.9 copy-start.4
  195.3 2.9 copy-start.6
  201.3 73.2 %all-to-all-start.4 = ((bf16[64,16,1280]{2,1,0:T(8,128)(2,1)}), bf16[64,16,1280]{2,1,0:T(8,128)(2,1)}, u32[]{:S(2)}, u32[]{:S(2)}) async-start(bf16[64,16,1280]{2,1,0:T(8,128)(2,1)} %bitcast.77), calls=%async_computation.5 | async-start | bytes 5242880 | tf_op jit(solution)/shard_map/all_to_all | solution.py:121
Sparse Core Ops, SparseCore 0:
  152.3 42.9 all-reduce.1
  198.1 100.5 reduce-scatter.1
where the time goes:
time: 313 us; the launch traced here: 311 us
  waiting for transfers between devices  195 us (62%)
  matrix products  52.4 us (17%)
  starting transfers between devices  40.7 us (13%)
  between operations  14.2 us (5%)
  other arithmetic  4.48 us (1%)
  local copies, waits for them, and re-layouts  3.48 us (1%)
    all_to_all x1, waiting for transfers between devices, local(): lax.all_to_all(place_rows(inputs), 'adapter', split_axis=0, concat_axis=0...  51.9 us
    all_to_all x1, waiting for transfers between devices, local(): lax.all_to_all(adapter_rows, 'adapter', split_axis=0, concat_axis=0, tile...  50.9 us
    psum x1, waiting for transfers between devices, local(): summed_gradient = lax.psum(stacked, 'tensor')  32.5 us
    reduce_scatter x1, waiting for transfers between devices, local(): lax.psum_scatter(partial_grad, 'tensor', scatter_dimension=1, tiled=True)  24.2 us
    dot_general x5, matrix products, contract_token_rows(): lax.dot_general(left, right, (((0,), (0,)), ((), ())), preferred_element_...  16.7 us
    all_to_all x1, waiting for transfers between devices, local(): lax.all_to_all(place_rows(grad_value), 'adapter', split_axis=0, concat_ax...  16.4 us
    all_to_all x1, waiting for transfers between devices, local(): lax.all_to_all(place_rows(grad_key), 'adapter', split_axis=0, concat_axis...  13.1 us
    all_to_all x1, starting transfers between devices, local(): lax.all_to_all(place_rows(local_hot), 'adapter', split_axis=0, concat_axi...  12.1 us
  transfers between devices with their start and end apart: 7, of which 7 were waited for; matrix products, arithmetic and copies ran while one was open for 15% of the time, Pallas kernels for 0%

commit v1 on v0

v1 whole, which is shorter than its diff:
```python
import functools

import jax
import jax.numpy as jnp
from jax import lax
from jax.experimental import pallas as pl
from jax.experimental.pallas import tpu as pltpu
from jax.sharding import PartitionSpec as P

adapter_scale = 2.0

SLOTS = 16
MIB = 1 << 20
bf16 = jnp.bfloat16
f32 = jnp.float32


def call(kernel, outs, name, vmem=48, smem=0, scratch=(), after=(), anywhere=False, alias={}):
    def run(*args):
        specs = [
            pl.BlockSpec(memory_space=pltpu.SMEM if i < smem else pl.ANY if anywhere else pltpu.VMEM)
            for i in range(len(args))
        ]
        specs += [pl.BlockSpec(memory_space=pl.ANY)] * len(after)

        def body(*refs):
            kernel(*refs[: len(args)], *refs[len(args) + len(after) :])

        return pl.pallas_call(
            body,
            out_shape=[jax.ShapeDtypeStruct(s, d) for s, d in outs],
            in_specs=specs,
            out_specs=[pl.BlockSpec(memory_space=pl.ANY if anywhere else pltpu.VMEM) for _ in outs],
            scratch_shapes=list(scratch),
            compiler_params=pltpu.CompilerParams(vmem_limit_bytes=vmem * MIB),
            input_output_aliases=alias,
            name=name,
        )(*args, *after)

    return run


def dot(a, b, ca, cb):
    return lax.dot_general(a, b, (((ca,), (cb,)), ((), ())), preferred_element_type=f32)


def route_kernel(ids_ref, key_ref, value_ref, route_ref, sent_ref):
    ids = ids_ref[...]
    tokens = ids.shape[1]
    slots = route_ref.shape[0]
    owner = ids >> 4
    within = ids & 15
    owner_hot = lax.broadcasted_iota(jnp.int32, (slots // SLOTS, tokens), 0) == owner
    earlier = lax.broadcasted_iota(jnp.int32, (tokens, tokens), 0) < lax.broadcasted_iota(
        jnp.int32, (tokens, tokens), 1
    )
    before = dot(owner_hot.astype(f32).astype(bf16), earlier.astype(f32).astype(bf16), 1, 0)
    rank = jnp.sum(jnp.where(owner_hot, before, 0.0), axis=0, keepdims=True).astype(jnp.int32)
    target = owner * SLOTS + rank
    route = (lax.broadcasted_iota(jnp.int32, (slots, tokens), 0) == target).astype(f32).astype(bf16)
    route_ref[...] = route
    kv = key_ref.shape[1]
    sent_ref[:, :kv] = dot(route, key_ref[...], 1, 0).astype(bf16)
    sent_ref[:, kv : 2 * kv] = dot(route, value_ref[...], 1, 0).astype(bf16)
    code = jnp.broadcast_to((within + 1).astype(f32), (128, tokens)).astype(bf16)
    sent_ref[:, 2 * kv :] = dot(route, code, 1, 1).astype(bf16)


def place_kernel(route_ref, inputs_ref, out_ref):
    out_ref[...] = dot(route_ref[...], inputs_ref[...], 1, 0).astype(bf16)


def weights_kernel(shifts, where_ref, weight_key_ref, weight_value_ref, *refs):
    outs, sems = refs[: len(shifts)], refs[-1]
    width, kv = outs[0].shape[0], weight_key_ref.shape[1]
    copies = []
    for i, s in enumerate(shifts):
        rows = pl.ds(pl.multiple_of(lax.rem(where_ref[3] + s, 4) * width, width), width)
        for j, ref in enumerate((weight_key_ref, weight_value_ref)):
            copies.append(
                pltpu.make_async_copy(
                    ref.at[rows, :], outs[i].at[:, j * kv : (j + 1) * kv], sems.at[2 * i + j]
                )
            )
    for copy in copies:
        copy.start()
    for copy in copies:
        copy.wait()


def pass_kernel(in_ref, out_ref):
    pass


def join_kernel(key_ref, value_ref, out_ref, sems):
    kv = key_ref.shape[1]
    first = pltpu.make_async_copy(key_ref, out_ref.at[:, :kv], sems.at[0])
    second = pltpu.make_async_copy(value_ref, out_ref.at[:, kv:], sems.at[1])
    first.start()
    second.start()
    first.wait()
    second.wait()


def code_row(meta):
    pick = (lax.broadcasted_iota(jnp.int32, (8, 128), 1) == 0).astype(f32).astype(bf16)
    return dot(pick, meta, 1, 1)[:1].astype(jnp.int32)


def select(expanded, code, count, rank):
    total = jnp.where(code == 1, expanded[:rank], 0.0)
    for l in range(1, count):
        total = total + jnp.where(code == l + 1, expanded[l * rank : (l + 1) * rank], 0.0)
    return total


def spread(values, code, count):
    wide = values.astype(f32)
    return jnp.concatenate(
        [jnp.where(code == l + 1, wide, 0.0).astype(bf16) for l in range(count)], axis=0
    )


def back_kernel(got_ref, up_key_ref, up_value_ref, part_ref, code_ref):
    kv = up_key_ref.shape[1]
    code = code_row(got_ref[:, 2 * kv :])
    code_ref[...] = jnp.broadcast_to(code, code_ref.shape)
    part_ref[:16] = select(dot(up_key_ref[...], got_ref[:, :kv], 1, 1), code, 16, 16)
    part_ref[16:] = select(dot(up_value_ref[...], got_ref[:, kv : 2 * kv], 1, 1), code, 16, 16)


def lora_kernel(code_ref, a_ref, b_ref, c_ref, d_ref, down_key_ref, down_value_ref, rows_ref, back_ref):
    code = code_ref[:1]
    total = (a_ref[...] + c_ref[...]) + (b_ref[...] + d_ref[...])
    back = (adapter_scale * total).astype(bf16)
    back_ref[...] = back
    rows = dot(spread(back[:16], code, 16), down_key_ref[...], 0, 0)
    rows = rows + dot(spread(back[16:], code, 16), down_value_ref[...], 0, 0)
    rows_ref[...] = rows.astype(bf16)


def low_kernel(code_ref, rows_ref, down_key_ref, down_value_ref, part_ref):
    code = code_ref[:1]
    part_ref[:16] = select(dot(down_key_ref[...], rows_ref[...], 1, 1), code, 16, 16)
    part_ref[16:] = select(dot(down_value_ref[...], rows_ref[...], 1, 1), code, 16, 16)


def grads_kernel(code_ref, back_ref, a_ref, b_ref, c_ref, d_ref, rows_ref, got_ref,
                 down_key_out, down_value_out, up_key_out, up_value_out):
    code = code_ref[:1]
    kv = up_key_out.shape[1]
    low = ((a_ref[...] + c_ref[...]) + (b_ref[...] + d_ref[...])).astype(bf16)
    down_key_out[...] = dot(spread(back_ref[:16], code, 16), rows_ref[...], 1, 0)
    down_value_out[...] = dot(spread(back_ref[16:], code, 16), rows_ref[...], 1, 0)
    up_key_out[...] = adapter_scale * dot(spread(low[:16], code, 16), got_ref[:, :kv], 1, 0)
    up_value_out[...] = adapter_scale * dot(
        spread(low[16:], code, 16), got_ref[:, kv : 2 * kv], 1, 0
    )


def frozen_kernel(g0, g1, g2, g3, w0, w1, w2, w3, out_ref):
    total = dot(g0[...], w0[...], 1, 1)
    total = total + dot(g1[...], w1[...], 1, 1)
    total = total + dot(g2[...], w2[...], 1, 1)
    out_ref[...] = total + dot(g3[...], w3[...], 1, 1)


def final_kernel(route_ref, rows_ref, frozen_ref, out_ref):
    out_ref[...] = (frozen_ref[...] + dot(route_ref[...], rows_ref[...], 0, 0)).astype(bf16)


def shift_tensor(x, s):
    return lax.ppermute(x, "tensor", [(i, (i + s) % 4) for i in range(4)])


def local(inputs, grad_key, grad_value, weight_key, weight_value, down_key, down_value,
          up_key, up_value, adapter_ids):
    tokens, width = inputs.shape
    kv = grad_key.shape[1]
    owners, rank = 64, down_key.shape[1]
    lr = down_key.shape[0] * rank
    slots = owners * SLOTS
    me = lax.axis_index("adapter")
    t = lax.axis_index("tensor")
    where = jnp.stack([me // 8, me // 2 % 4, me % 2, t]).astype(jnp.int32)
    down_key, down_value = down_key.reshape(lr, width), down_value.reshape(lr, width)
    up_key, up_value = up_key.reshape(lr, kv), up_value.reshape(lr, kv)

    route, sent = call(
        route_kernel, [((slots, tokens), bf16), ((slots, 2 * kv + 128), bf16)], "route"
    )(adapter_ids.reshape(1, tokens), grad_key, grad_value)
    got = lax.all_to_all(sent, "adapter", split_axis=0, concat_axis=0, tiled=True)

    (placed,) = call(place_kernel, [((slots, width), bf16)], "place")(route, inputs)
    held = lax.all_to_all(placed, "adapter", split_axis=0, concat_axis=0, tiled=True)

    def weights(shifts, after=()):
        sliced = call(
            functools.partial(weights_kernel, shifts),
            [((width, 2 * kv), bf16)] * len(shifts), "weights", smem=1, anywhere=True,
            scratch=[pltpu.SemaphoreType.DMA((2 * len(shifts),))], after=after,
        )(where, weight_key, weight_value)
        return {s: shift_tensor(x, s) if s else x for s, x in zip(shifts, sliced)}

    blocks = weights((1, 3))
    part, code = call(
        back_kernel, [((2 * rank, slots), f32), ((8, slots), jnp.int32)], "back",
        after=[blocks[1], blocks[3]],
    )(got, up_key, up_value)
    sums = [part] + [shift_tensor(part, s) for s in (1, 2, 3)]
    rows, back = call(
        lora_kernel, [((slots, width), bf16), ((2 * rank, slots), bf16)], "lora",
    )(code, *sums, down_key, down_value)
    (rows,) = call(pass_kernel, [((slots, width), bf16)], "pass", anywhere=True, alias={0: 0},
                   after=[held])(rows)
    returned = lax.all_to_all(rows, "adapter", split_axis=0, concat_axis=0, tiled=True)

    blocks |= weights((0, 2), after=[back])
    (both,) = call(
        join_kernel, [((tokens, 2 * kv), bf16)], "join", anywhere=True,
        scratch=[pltpu.SemaphoreType.DMA((2,))], after=[back],
    )(grad_key, grad_value)
    every = [both] + [shift_tensor(both, s) for s in (1, 2, 3)]
    (frozen,) = call(frozen_kernel, [((tokens, width), f32)], "frozen")(
        *every, *[blocks[s] for s in range(4)]
    )

    (part,) = call(low_kernel, [((2 * rank, slots), f32)], "low")(code, held, down_key, down_value)
    sums = [part] + [shift_tensor(part, s) for s in (1, 2, 3)]
    grads = call(
        grads_kernel, [((lr, width), f32)] * 2 + [((lr, kv), f32)] * 2, "grads"
    )(code, back, *sums, held, got)
    (input_gradient,) = call(final_kernel, [((tokens, width), bf16)], "final")(
        route, returned, frozen
    )
    count = lr // rank
    return (
        input_gradient,
        grads[0].reshape(count, rank, width),
        grads[1].reshape(count, rank, width),
        grads[2].reshape(count, rank, kv),
        grads[3].reshape(count, rank, kv),
    )


def solution(mesh):
    wide = P("adapter", "tensor")
    frozen = P(None, "tensor")
    adapter = P("adapter", None, "tensor")
    return jax.shard_map(
        local,
        mesh=mesh,
        in_specs=(wide, wide, wide, frozen, frozen, adapter, adapter, adapter, adapter, P("adapter")),
        out_specs=(wide, adapter, adapter, adapter, adapter),
        check_vma=False,
    )
```

time: 313 us -> 208 us (0.66)
  waiting for transfers between devices: 195 us -> 110 us
  matrix products: 52.4 us -> 0 us
  Pallas kernels: 0 us -> 24.3 us
  local copies, waits for them, and re-layouts: 3.48 us -> 20.1 us
  between operations: 14.2 us -> 0.91 us
  starting transfers between devices: 40.7 us -> 52.3 us
  other arithmetic: 4.48 us -> 0.08 us
    all_to_all x5 -> x3, waiting for transfers between devices: 139 us -> 39.9 us  [the longest x1 28.8 us: local(): lax.all_to_all(sent, 'adapter', split_axis=0, concat_axis=0, tiled=True)]
    ppermute x0 -> x12, waiting for transfers between devices: none -> 69.8 us  [shift_tensor(): return lax.ppermute(x, 'tensor', [(i, (i + s) % 4) for i in range(4)])]
    dot_general x17 -> x0, matrix products: 52.4 us -> none  [the longest x5 16.7 us: contract_token_rows(): lax.dot_general(left, right, (((0,), (0,)), ((), ())), preferred_element_...]
    psum x1 -> x0, waiting for transfers between devices: 32.5 us -> none  [local(): summed_gradient = lax.psum(stacked, 'tensor')]
    ppermute x0 -> x12, starting transfers between devices: none -> 29.1 us  [shift_tensor(): return lax.ppermute(x, 'tensor', [(i, (i + s) % 4) for i in range(4)])]
    pallas_call x0 -> x12, Pallas kernels: none -> 24.3 us  [run(): pl.pallas_call(body, out_shape=[jax.ShapeDtypeStruct(s, d) for s, d in ou...]
    reduce_scatter x1 -> x0, waiting for transfers between devices: 24.2 us -> none  [local(): lax.psum_scatter(partial_grad, 'tensor', scatter_dimension=1, tiled=True)]
    unnamed x16 -> x54, local copies, waits for them, and re-layouts: 1.03 us -> 20.1 us
  transfers between devices with their start and end apart: 7 -> 15, of which waited for: 7 -> 7; matrix products, arithmetic and copies ran while one was open for 15% -> 0% of each run, Pallas kernels for 0% -> 9%
where the time goes in v1:
time: 208 us; the launch traced here: 207 us
  waiting for transfers between devices  110 us (53%)
  starting transfers between devices  52.3 us (25%)
  Pallas kernels  24.3 us (12%)
  local copies, waits for them, and re-layouts  20.1 us (10%)
    ppermute x12, waiting for transfers between devices, shift_tensor(): return lax.ppermute(x, 'tensor', [(i, (i + s) % 4) for i in range(4)])  69.8 us
    ppermute x12, starting transfers between devices, shift_tensor(): return lax.ppermute(x, 'tensor', [(i, (i + s) % 4) for i in range(4)])  29.1 us
    all_to_all x1, waiting for transfers between devices, local(): lax.all_to_all(sent, 'adapter', split_axis=0, concat_axis=0, tiled=True)  28.8 us
    pallas_call x12, Pallas kernels, run(): pl.pallas_call(body, out_shape=[jax.ShapeDtypeStruct(s, d) for s, d in ou...  24.3 us
    unnamed x54, local copies, waits for them, and re-layouts  20.1 us
    all_to_all x1, starting transfers between devices, local(): lax.all_to_all(sent, 'adapter', split_axis=0, concat_axis=0, tiled=True)  12.1 us
    all_to_all x1, waiting for transfers between devices, local(): lax.all_to_all(placed, 'adapter', split_axis=0, concat_axis=0, tiled=True)  11.1 us
    all_to_all x1, starting transfers between devices, local(): lax.all_to_all(rows, 'adapter', split_axis=0, concat_axis=0, tiled=True)  5.6 us
  transfers between devices with their start and end apart: 15, of which 7 were waited for; matrix products, arithmetic and copies ran while one was open for 0% of the time, Pallas kernels for 9%

profile of v1, /device:TPU:8, one launch (start us, length us, event | category | flops | bytes accessed | tf_op | source)
XLA Modules:
  0.0 207.4 jit_solution(476589529848615387)
XLA Ops:
  0.6 0.9 copy-done.20
  1.6 0.9 copy-done.22
  2.5 0.7 copy-done.26
  3.2 1.3 route.1
  4.6 1.0 copy-done.18
  5.6 1.0 copy-done.12
  6.7 12.1 %all-to-all-start = ((bf16[64,16,640]{2,1,0:T(8,128)(2,1)}), bf16[64,16,640]{2,1,0:T(8,128)(2,1)S(1)}, u32[]{:S(2)}, u32[]{:S(2)}) async-start(bf16[64,16,640]{2,1,0:T(8,128)(2,1)} %bitcast.30), calls=%async_computation | async-start | bytes 2621440 | tf_op jit(solution)/shard_map/all_to_all | solution.py:192
  18.8 1.2 copy-done.13
  20.0 1.3 copy-done.19
  21.3 1.5 place.1
  22.9 1.5 copy-done.3
  24.4 28.8 %all-to-all-done = bf16[64,16,640]{2,1,0:T(8,128)(2,1)S(1)} async-done(((bf16[64,16,640]{2,1,0:T(8,128)(2,1)}), bf16[64,16,640]{2,1,0:T(8,128)(2,1)S(1)}, u32[]{:S(2)}, u32[]{:S(2)}) %all-to-all-start) | async-done | bytes 1310752 | tf_op jit(solution)/shard_map/all_to_all | solution.py:192
  53.2 1.1 copy-done
  54.3 5.5 %all-to-all-start.1 = ((bf16[64,16,1280]{2,1,0:T(8,128)(2,1)}), bf16[64,16,1280]{2,1,0:T(8,128)(2,1)S(1)}, u32[]{:S(2)}, u32[]{:S(2)}) async-start(bf16[64,16,1280]{2,1,0:T(8,128)(2,1)} %bitcast.24), calls=%async_computation.1 | async-start | bytes 5242880 | tf_op jit(solution)/shard_map/all_to_all | solution.py:195
  59.9 1.7 copy-done.4
  61.7 1.9 weights.2
  63.6 1.6 collective-permute-start
  65.2 1.7 collective-permute-start.1
  66.9 28.8 %collective-permute-done.refs_3_.refs_5_ = bf16[1280,512]{1,0:T(8,128)(2,1)S(1)} collective-permute-done((bf16[1280,512]{1,0:T(8,128)(2,1)S(1)}, bf16[1280,512]{1,0:T(8,128)(2,1)S(1)}, u32[]{:S(2)}, u32[]{:S(2)}) %collective-permute-start) | collective-permute-done | bytes 1310752 | tf_op jit(solution)/shard_map/ppermute | solution.py:173
  95.8 0.6 back.1
  96.3 0.4 copy-done.9
  96.8 0.4 copy-done.11
  97.2 2.5 %collective-permute-start.4 = (f32[32,1024]{1,0:T(8,128)S(1)}, f32[32,1024]{1,0:T(8,128)S(1)}, u32[]{:S(2)}, u32[]{:S(2)}) collective-permute-start(f32[32,1024]{1,0:T(8,128)S(1)} %get-tuple-element.24.refs_1_), channel_id=1, source_target_pairs={{0,3},{1,0},{2,1},{3,2},{4,7},{5,4},{6,5},{7,6},{8,11},{9,8},{10,9... | collective-permute-start | bytes 393224 | tf_op jit(solution)/shard_map/ppermute | solution.py:173
  99.7 0.6 collective-permute-start.3
  100.3 0.6 collective-permute-start.2
  100.9 3.6 %collective-permute-done.4.refs_4_ = f32[32,1024]{1,0:T(8,128)S(1)} collective-permute-done((f32[32,1024]{1,0:T(8,128)S(1)}, f32[32,1024]{1,0:T(8,128)S(1)}, u32[]{:S(2)}, u32[]{:S(2)}) %collective-permute-start.4) | collective-permute-done | bytes 131104 | tf_op jit(solution)/shard_map/ppermute | solution.py:173
  104.5 2.3 %collective-permute-done.3.refs_3_ = f32[32,1024]{1,0:T(8,128)S(1)} collective-permute-done((f32[32,1024]{1,0:T(8,128)S(1)}, f32[32,1024]{1,0:T(8,128)S(1)}, u32[]{:S(2)}, u32[]{:S(2)}) %collective-permute-start.3) | collective-permute-done | bytes 131104 | tf_op jit(solution)/shard_map/ppermute | solution.py:173
  106.8 1.3 collective-permute-done.2.refs_2_
  108.2 1.6 lora.1
  109.8 1.5 copy-done.6
  111.2 11.1 %all-to-all-done.1 = bf16[64,16,1280]{2,1,0:T(8,128)(2,1)S(1)} async-done(((bf16[64,16,1280]{2,1,0:T(8,128)(2,1)}), bf16[64,16,1280]{2,1,0:T(8,128)(2,1)S(1)}, u32[]{:S(2)}, u32[]{:S(2)}) %all-to-all-start.1) | async-done | bytes 2621472 | tf_op jit(solution)/shard_map/all_to_all | solution.py:195
  122.3 1.7 copy-done.7
  124.0 1.5 copy-done.8
  125.5 5.6 %all-to-all-start.2 = ((bf16[64,16,1280]{2,1,0:T(8,128)(2,1)}), bf16[64,16,1280]{2,1,0:T(8,128)(2,1)}, u32[]{:S(2)}, u32[]{:S(2)}) async-start(bf16[64,16,1280]{2,1,0:T(8,128)(2,1)} %bitcast.25), calls=%async_computation.2 | async-start | bytes 5242880 | tf_op jit(solution)/shard_map/all_to_all | solution.py:216
  131.2 1.7 copy-done.5
  132.9 1.9 weights.3
  134.8 3.3 %collective-permute-start.8 = (bf16[1280,512]{1,0:T(8,128)(2,1)S(1)}, bf16[1280,512]{1,0:T(8,128)(2,1)S(1)}, u32[]{:S(2)}, u32[]{:S(2)}) collective-permute-start(bf16[1280,512]{1,0:T(8,128)(2,1)S(1)} %get-tuple-element.28), channel_id=1, source_target_pairs={{0,2},{1,3},{2,0},{3,1},{4,6},{5,7},{6,4},{7,5},{8,10},{9,11},{10,... | collective-permute-start | bytes 3932168 | tf_op jit(solution)/shard_map/ppermute | solution.py:173
  138.2 1.2 collective-permute-start.7
  139.4 1.5 collective-permute-start.6
  141.0 1.6 low.1.refs_2_
  142.5 3.3 %collective-permute-start.11 = (f32[32,1024]{1,0:T(8,128)S(1)}, f32[32,1024]{1,0:T(8,128)S(1)}, u32[]{:S(2)}, u32[]{:S(2)}) collective-permute-start(f32[32,1024]{1,0:T(8,128)S(1)} %low.1.refs_2_), channel_id=1, source_target_pairs={{0,3},{1,0},{2,1},{3,2},{4,7},{5,4},{6,5},{7,6},{8,11},{9,8},{10,9... | collective-permute-start | bytes 393224 | tf_op jit(solution)/shard_map/ppermute | solution.py:173
  145.8 33.8 %collective-permute-done.7.refs_3_ = bf16[512,512]{1,0:T(8,128)(2,1)S(1)} collective-permute-done((bf16[512,512]{1,0:T(8,128)(2,1)S(1)}, bf16[512,512]{1,0:T(8,128)(2,1)S(1)}, u32[]{:S(2)}, u32[]{:S(2)}) %collective-permute-start.7) | collective-permute-done | bytes 524320 | tf_op jit(solution)/shard_map/ppermute | solution.py:173
  179.6 2.0 collective-permute-start.10
  181.6 10.7 %collective-permute-start.9 = (f32[32,1024]{1,0:T(8,128)S(1)}, f32[32,1024]{1,0:T(8,128)S(1)}, u32[]{:S(2)}, u32[]{:S(2)}) collective-permute-start(f32[32,1024]{1,0:T(8,128)S(1)} %low.1.refs_2_), channel_id=1, source_target_pairs={{0,1},{1,2},{2,3},{3,0},{4,5},{5,6},{6,7},{7,4},{8,9},{9,10},{10,1... | collective-permute-start | bytes 393224 | tf_op jit(solution)/shard_map/ppermute | solution.py:173
  192.3 5.9 %frozen.1.refs_2_ = f32[512,1280]{1,0:T(8,128)} custom-call(bf16[512,512]{1,0:T(8,128)(2,1)S(1)} %join.1.refs_0_, bf16[512,512]{1,0:T(8,128)(2,1)S(1)} %collective-permute-done.5.refs_1_, bf16[512,512]{1,0:T(8,128)(2,1)S(1)} %collective-permute-done.6.refs_2_, bf16[512,512]{1,0:T(8,128)(2,1)S(1)} %collective-permute-done.7.refs_3_, ...), custom_call_target="tpu_custom_call" | custom-call | tf_op jit(solution)/shard_map/frozen/pallas_call | solution.py:29
  198.2 2.8 %grads.1 = (f32[256,1280]{1,0:T(8,128)}, f32[256,1280]{1,0:T(8,128)}, f32[256,256]{1,0:T(8,128)}, f32[256,256]{1,0:T(8,128)}) custom-call(s32[8,1024]{1,0:T(8,128)S(1)} %get-tuple-element.23.refs_0_, bf16[32,1024]{1,0:T(8,128)(2,1)S(1)} %get-tuple-element.26.refs_2_.refs_3_.refs_1_, f32[32,1024]{1,0:T(8,128)S(1)} %low.1.refs_2_, ...), custom_call_target="tpu_custom_call" | custom-call | tf_op jit(solution)/shard_map/grads/pallas_call | solution.py:29
  201.0 1.2 copy-done.14
  202.2 5.2 %final.1 = bf16[512,1280]{1,0:T(8,128)(2,1)} custom-call(bf16[1024,512]{1,0:T(8,128)(2,1)S(1)} %copy-done.14, bf16[1024,1280]{1,0:T(8,128)(2,1)} %bitcast.14.refs_1_, f32[512,1280]{1,0:T(8,128)} %frozen.1.refs_2_), custom_call_target="tpu_custom_call" | custom-call | tf_op jit(solution)/shard_map/final/pallas_call | solution.py:29
  (49 shorter events, 0.3 us)
Async XLA Ops:
  0.6 1.0 copy-start.20
  1.6 0.9 copy-start.22
  2.5 0.7 copy-start.26
  4.6 1.1 copy-start.18
  5.6 1.0 copy-start.12
  6.7 46.5 %all-to-all-start = ((bf16[64,16,640]{2,1,0:T(8,128)(2,1)}), bf16[64,16,640]{2,1,0:T(8,128)(2,1)S(1)}, u32[]{:S(2)}, u32[]{:S(2)}) async-start(bf16[64,16,640]{2,1,0:T(8,128)(2,1)} %bitcast.30), calls=%async_computation | async-start | bytes 2621440 | tf_op jit(solution)/shard_map/all_to_all | solution.py:192
  18.8 1.2 copy-start.13
  20.0 1.3 copy-start.19
  22.9 1.5 copy-start.3
  53.2 1.1 copy-start
  54.3 68.0 %all-to-all-start.1 = ((bf16[64,16,1280]{2,1,0:T(8,128)(2,1)}), bf16[64,16,1280]{2,1,0:T(8,128)(2,1)S(1)}, u32[]{:S(2)}, u32[]{:S(2)}) async-start(bf16[64,16,1280]{2,1,0:T(8,128)(2,1)} %bitcast.24), calls=%async_computation.1 | async-start | bytes 5242880 | tf_op jit(solution)/shard_map/all_to_all | solution.py:195
  59.9 1.7 copy-start.4
  61.6 34.1 %copy-start.1 = (bf16[64,16,640]{2,1,0:T(8,128)(2,1)S(1)}, bf16[64,16,640]{2,1,0:T(8,128)(2,1)}, u32[]{:S(2)}) copy-start(bf16[64,16,640]{2,1,0:T(8,128)(2,1)} %copy-done) | copy-start | bytes 3932164
  61.6 34.1 %copy-start.24 = (bf16[16,16,256]{2,1,0:T(8,128)(2,1)S(1)}, bf16[16,16,256]{2,1,0:T(8,128)(2,1)}, u32[]{:S(2)}) copy-start(bf16[16,16,256]{2,1,0:T(8,128)(2,1)} %param.17) | copy-start | bytes 393220
  61.7 34.1 %copy-start.25 = (bf16[16,16,256]{2,1,0:T(8,128)(2,1)S(1)}, bf16[16,16,256]{2,1,0:T(8,128)(2,1)}, u32[]{:S(2)}) copy-start(bf16[16,16,256]{2,1,0:T(8,128)(2,1)} %param.18) | copy-start | bytes 393220
  63.6 32.1 %collective-permute-start = (bf16[1280,512]{1,0:T(8,128)(2,1)S(1)}, bf16[1280,512]{1,0:T(8,128)(2,1)S(1)}, u32[]{:S(2)}, u32[]{:S(2)}) collective-permute-start(bf16[1280,512]{1,0:T(8,128)(2,1)S(1)} %get-tuple-element.21), channel_id=1, source_target_pairs={{0,1},{1,2},{2,3},{3,0},{4,5},{5,6},{6,7},{7,4},{8,9},{9,10},{10,1... | collective-permute-start | bytes 3932168 | tf_op jit(solution)/shard_map/ppermute | solution.py:173
  65.2 30.6 %collective-permute-start.1 = (bf16[1280,512]{1,0:T(8,128)(2,1)S(1)}, bf16[1280,512]{1,0:T(8,128)(2,1)S(1)}, u32[]{:S(2)}, u32[]{:S(2)}) collective-permute-start(bf16[1280,512]{1,0:T(8,128)(2,1)S(1)} %get-tuple-element.22), channel_id=1, source_target_pairs={{0,3},{1,0},{2,1},{3,2},{4,7},{5,4},{6,5},{7,6},{8,11},{9,8},{10,9... | collective-permute-start | bytes 3932168 | tf_op jit(solution)/shard_map/ppermute | solution.py:173
  95.7 1.1 copy-start.9
  95.7 1.5 copy-start.11
  95.7 12.4 %copy-start.15 = (bf16[16,16,1280]{2,1,0:T(8,128)(2,1)S(1)}, bf16[16,16,1280]{2,1,0:T(8,128)(2,1)}, u32[]{:S(2)}) copy-start(bf16[16,16,1280]{2,1,0:T(8,128)(2,1)} %param.15) | copy-start | bytes 1966084
  95.8 12.4 %copy-start.16 = (bf16[16,16,1280]{2,1,0:T(8,128)(2,1)S(1)}, bf16[16,16,1280]{2,1,0:T(8,128)(2,1)}, u32[]{:S(2)}) copy-start(bf16[16,16,1280]{2,1,0:T(8,128)(2,1)} %param.16) | copy-start | bytes 1966084
  97.2 7.3 %collective-permute-start.4 = (f32[32,1024]{1,0:T(8,128)S(1)}, f32[32,1024]{1,0:T(8,128)S(1)}, u32[]{:S(2)}, u32[]{:S(2)}) collective-permute-start(f32[32,1024]{1,0:T(8,128)S(1)} %get-tuple-element.24.refs_1_), channel_id=1, source_target_pairs={{0,3},{1,0},{2,1},{3,2},{4,7},{5,4},{6,5},{7,6},{8,11},{9,8},{10,9... | collective-permute-start | bytes 393224 | tf_op jit(solution)/shard_map/ppermute | solution.py:173
  99.7 7.1 %collective-permute-start.3 = (f32[32,1024]{1,0:T(8,128)S(1)}, f32[32,1024]{1,0:T(8,128)S(1)}, u32[]{:S(2)}, u32[]{:S(2)}) collective-permute-start(f32[32,1024]{1,0:T(8,128)S(1)} %get-tuple-element.24.refs_1_), channel_id=1, source_target_pairs={{0,2},{1,3},{2,0},{3,1},{4,6},{5,7},{6,4},{7,5},{8,10},{9,11},{10,... | collective-permute-start | bytes 393224 | tf_op jit(solution)/shard_map/ppermute | solution.py:173
  100.3 7.8 %collective-permute-start.2 = (f32[32,1024]{1,0:T(8,128)S(1)}, f32[32,1024]{1,0:T(8,128)S(1)}, u32[]{:S(2)}, u32[]{:S(2)}) collective-permute-start(f32[32,1024]{1,0:T(8,128)S(1)} %get-tuple-element.24.refs_1_), channel_id=1, source_target_pairs={{0,1},{1,2},{2,3},{3,0},{4,5},{5,6},{6,7},{7,4},{8,9},{9,10},{10,1... | collective-permute-start | bytes 393224 | tf_op jit(solution)/shard_map/ppermute | solution.py:173
  109.7 1.5 copy-start.6
  122.3 1.7 copy-start.7
  124.0 1.5 copy-start.8
  125.5 75.5 %all-to-all-start.2 = ((bf16[64,16,1280]{2,1,0:T(8,128)(2,1)}), bf16[64,16,1280]{2,1,0:T(8,128)(2,1)}, u32[]{:S(2)}, u32[]{:S(2)}) async-start(bf16[64,16,1280]{2,1,0:T(8,128)(2,1)} %bitcast.25), calls=%async_computation.2 | async-start | bytes 5242880 | tf_op jit(solution)/shard_map/all_to_all | solution.py:216
  131.1 1.7 copy-start.5
  132.9 5.2 %copy-start.21 = (bf16[512,256]{1,0:T(8,128)(2,1)S(1)}, bf16[512,256]{1,0:T(8,128)(2,1)}, u32[]{:S(2)}) copy-start(bf16[512,256]{1,0:T(8,128)(2,1)} %refs_0_.1) | copy-start | bytes 786436
  132.9 5.2 %copy-start.23 = (bf16[512,256]{1,0:T(8,128)(2,1)S(1)}, bf16[512,256]{1,0:T(8,128)(2,1)}, u32[]{:S(2)}) copy-start(bf16[512,256]{1,0:T(8,128)(2,1)} %refs_1_.8) | copy-start | bytes 786436
  134.8 6.1 %copy-start.17 = (bf16[16,16,1280]{2,1,0:T(8,128)(2,1)S(1)}, bf16[16,16,1280]{2,1,0:T(8,128)(2,1)}, u32[]{:S(2)}) copy-start(bf16[16,16,1280]{2,1,0:T(8,128)(2,1)} %param.16) | copy-start | bytes 1966084
  134.8 57.4 %collective-permute-start.8 = (bf16[1280,512]{1,0:T(8,128)(2,1)S(1)}, bf16[1280,512]{1,0:T(8,128)(2,1)S(1)}, u32[]{:S(2)}, u32[]{:S(2)}) collective-permute-start(bf16[1280,512]{1,0:T(8,128)(2,1)S(1)} %get-tuple-element.28), channel_id=1, source_target_pairs={{0,2},{1,3},{2,0},{3,1},{4,6},{5,7},{6,4},{7,5},{8,10},{9,11},{10,... | collective-permute-start | bytes 3932168 | tf_op jit(solution)/shard_map/ppermute | solution.py:173
  138.2 54.1 %copy-start.10 = (bf16[1280,512]{1,0:T(8,128)(2,1)S(1)}, bf16[1280,512]{1,0:T(8,128)(2,1)}, u32[]{:S(2)}) copy-start(bf16[1280,512]{1,0:T(8,128)(2,1)} %copy-done.9) | copy-start | bytes 3932164
  138.2 41.4 %collective-permute-start.7 = (bf16[512,512]{1,0:T(8,128)(2,1)S(1)}, bf16[512,512]{1,0:T(8,128)(2,1)S(1)}, u32[]{:S(2)}, u32[]{:S(2)}) collective-permute-start(bf16[512,512]{1,0:T(8,128)(2,1)S(1)} %join.1.refs_0_), channel_id=1, source_target_pairs={{0,3},{1,0},{2,1},{3,2},{4,7},{5,4},{6,5},{7,6},{8,11},{9,8},{10,9... | collective-permute-start | bytes 1572872 | tf_op jit(solution)/shard_map/ppermute | solution.py:173
  139.4 42.2 %collective-permute-start.6 = (bf16[512,512]{1,0:T(8,128)(2,1)S(1)}, bf16[512,512]{1,0:T(8,128)(2,1)S(1)}, u32[]{:S(2)}, u32[]{:S(2)}) collective-permute-start(bf16[512,512]{1,0:T(8,128)(2,1)S(1)} %join.1.refs_0_), channel_id=1, source_target_pairs={{0,2},{1,3},{2,0},{3,1},{4,6},{5,7},{6,4},{7,5},{8,10},{9,11},{10,... | collective-permute-start | bytes 1572872 | tf_op jit(solution)/shard_map/ppermute | solution.py:173
  141.0 51.3 %collective-permute-start.5 = (bf16[512,512]{1,0:T(8,128)(2,1)S(1)}, bf16[512,512]{1,0:T(8,128)(2,1)S(1)}, u32[]{:S(2)}, u32[]{:S(2)}) collective-permute-start(bf16[512,512]{1,0:T(8,128)(2,1)S(1)} %join.1.refs_0_), channel_id=1, source_target_pairs={{0,1},{1,2},{2,3},{3,0},{4,5},{5,6},{6,7},{7,4},{8,9},{9,10},{10,1... | collective-permute-start | bytes 1572872 | tf_op jit(solution)/shard_map/ppermute | solution.py:173
  142.5 55.6 %collective-permute-start.11 = (f32[32,1024]{1,0:T(8,128)S(1)}, f32[32,1024]{1,0:T(8,128)S(1)}, u32[]{:S(2)}, u32[]{:S(2)}) collective-permute-start(f32[32,1024]{1,0:T(8,128)S(1)} %low.1.refs_2_), channel_id=1, source_target_pairs={{0,3},{1,0},{2,1},{3,2},{4,7},{5,4},{6,5},{7,6},{8,11},{9,8},{10,9... | collective-permute-start | bytes 393224 | tf_op jit(solution)/shard_map/ppermute | solution.py:173
  179.6 18.6 %collective-permute-start.10 = (f32[32,1024]{1,0:T(8,128)S(1)}, f32[32,1024]{1,0:T(8,128)S(1)}, u32[]{:S(2)}, u32[]{:S(2)}) collective-permute-start(f32[32,1024]{1,0:T(8,128)S(1)} %low.1.refs_2_), channel_id=1, source_target_pairs={{0,2},{1,3},{2,0},{3,1},{4,6},{5,7},{6,4},{7,5},{8,10},{9,11},{10,... | collective-permute-start | bytes 393224 | tf_op jit(solution)/shard_map/ppermute | solution.py:173
  181.6 16.6 %collective-permute-start.9 = (f32[32,1024]{1,0:T(8,128)S(1)}, f32[32,1024]{1,0:T(8,128)S(1)}, u32[]{:S(2)}, u32[]{:S(2)}) collective-permute-start(f32[32,1024]{1,0:T(8,128)S(1)} %low.1.refs_2_), channel_id=1, source_target_pairs={{0,1},{1,2},{2,3},{3,0},{4,5},{5,6},{6,7},{7,4},{8,9},{9,10},{10,1... | collective-permute-start | bytes 393224 | tf_op jit(solution)/shard_map/ppermute | solution.py:173
  192.3 5.9 %copy-start.2 = (bf16[64,16,640]{2,1,0:T(8,128)(2,1)S(1)}, bf16[64,16,640]{2,1,0:T(8,128)(2,1)}, u32[]{:S(2)}) copy-start(bf16[64,16,640]{2,1,0:T(8,128)(2,1)} %copy-done) | copy-start | bytes 3932164
  201.0 1.2 copy-start.14

commit v2 on v1

v2 whole, which is shorter than its diff:
```python
import functools

import jax
import jax.numpy as jnp
from jax import lax
from jax.experimental import pallas as pl
from jax.experimental.pallas import tpu as pltpu
from jax.sharding import PartitionSpec as P

adapter_scale = 2.0

SLOTS = 16
MIB = 1 << 20
bf16 = jnp.bfloat16
f32 = jnp.float32


def move(pairs, sem):
    copies = [pltpu.make_async_copy(a, b, sem.at[i]) for i, (a, b) in enumerate(pairs)]
    for copy in copies:
        copy.start()
    for copy in copies:
        copy.wait()


def call(kernel, outs, name, vmem=56, smem=0, scratch=(), after=(), staged=True, loose=()):
    def run(*args):
        count, first = len(args), len(args) + len(after)
        specs = [
            pl.BlockSpec(
                memory_space=pltpu.SMEM if i < smem else pl.ANY if i in loose else pltpu.HBM
            )
            for i in range(count)
        ]
        specs += [pl.BlockSpec(memory_space=pl.ANY)] * len(after)
        held = [pltpu.VMEM(arg.shape, arg.dtype) for arg in args[smem:]] if staged else []
        made = [pltpu.VMEM(s, d) for s, d in outs]
        sems = [pltpu.SemaphoreType.DMA((max(len(held), len(made)),))]

        def body(*refs):
            ins, rest, sem = refs[:count], refs[first:-1], refs[-1]
            results, rest = rest[: len(outs)], rest[len(outs) :]
            results_held, rest = rest[: len(outs)], rest[len(outs) :]
            if staged:
                places, rest = rest[: len(held)], rest[len(held) :]
                move(list(zip(ins[smem:], places)), sem)
                ins = ins[:smem] + places
            kernel(*ins, *results_held, *rest)
            move(list(zip(results_held, results)), sem)

        return pl.pallas_call(
            body,
            out_shape=[jax.ShapeDtypeStruct(s, d) for s, d in outs],
            in_specs=specs,
            out_specs=[pl.BlockSpec(memory_space=pltpu.HBM) for _ in outs],
            scratch_shapes=made + held + list(scratch) + sems,
            compiler_params=pltpu.CompilerParams(vmem_limit_bytes=vmem * MIB),
            name=name,
        )(*args, *after)

    return run


def dot(a, b, ca, cb):
    return lax.dot_general(a, b, (((ca,), (cb,)), ((), ())), preferred_element_type=f32)


def route_kernel(ids_ref, key_ref, value_ref, target_ref, sent_ref):
    ids = ids_ref[...]
    tokens = ids.shape[1]
    slots = sent_ref.shape[0]
    owner = ids >> 4
    within = ids & 15
    owner_hot = lax.broadcasted_iota(jnp.int32, (slots // SLOTS, tokens), 0) == owner
    earlier = lax.broadcasted_iota(jnp.int32, (tokens, tokens), 0) < lax.broadcasted_iota(
        jnp.int32, (tokens, tokens), 1
    )
    before = dot(owner_hot.astype(f32).astype(bf16), earlier.astype(f32).astype(bf16), 1, 0)
    rank = jnp.sum(jnp.where(owner_hot, before, 0.0), axis=0, keepdims=True).astype(jnp.int32)
    target = owner * SLOTS + rank
    target_ref[...] = jnp.broadcast_to(target, target_ref.shape)
    route = routing(target, slots)
    kv = key_ref.shape[1]
    sent_ref[:, :kv] = dot(route, key_ref[...], 1, 0).astype(bf16)
    sent_ref[:, kv : 2 * kv] = dot(route, value_ref[...], 1, 0).astype(bf16)
    code = jnp.broadcast_to((within + 1).astype(f32), (128, tokens)).astype(bf16)
    sent_ref[:, 2 * kv :] = dot(route, code, 1, 1).astype(bf16)


def routing(target, slots):
    place = lax.broadcasted_iota(jnp.int32, (slots, target.shape[1]), 0)
    return (place == target).astype(f32).astype(bf16)


def place_kernel(target_ref, inputs_ref, out_ref, back_ref):
    route = routing(target_ref[:1], out_ref.shape[0])
    out_ref[...] = dot(route, inputs_ref[...], 1, 0).astype(bf16)
    back_ref[...] = route.T


def weights_kernel(shifts, where_ref, weight_key_ref, weight_value_ref, *refs):
    outs, sem = refs[: len(shifts)], refs[-1]
    width, kv = outs[0].shape[0], weight_key_ref.shape[1]
    pairs = []
    for s, out in zip(shifts, outs):
        rows = pl.ds(pl.multiple_of(((where_ref[0] + s) & 3) * width, width), width)
        pairs.append((weight_key_ref.at[rows, :], out.at[:, :kv]))
        pairs.append((weight_value_ref.at[rows, :], out.at[:, kv:]))
    move(pairs, sem)


def join_kernel(key_ref, value_ref, out_ref):
    kv = key_ref.shape[1]
    out_ref[:, :kv] = key_ref[...]
    out_ref[:, kv:] = value_ref[...]


def code_row(meta):
    pick = (lax.broadcasted_iota(jnp.int32, (8, 128), 1) == 0).astype(f32).astype(bf16)
    return dot(pick, meta, 1, 1)[:1].astype(jnp.int32)


def select(expanded, code, count, rank):
    total = jnp.where(code == 1, expanded[:rank], 0.0)
    for l in range(1, count):
        total = total + jnp.where(code == l + 1, expanded[l * rank : (l + 1) * rank], 0.0)
    return total


def spread(values, code, count):
    wide = values.astype(f32)
    return jnp.concatenate(
        [jnp.where(code == l + 1, wide, 0.0).astype(bf16) for l in range(count)], axis=0
    )


def back_kernel(got_ref, up_key_ref, up_value_ref, part_ref, code_ref, kept_ref):
    kv = up_key_ref.shape[1]
    kept_ref[...] = got_ref[:, : 2 * kv]
    code = code_row(got_ref[:, 2 * kv :])
    code_ref[...] = jnp.broadcast_to(code, code_ref.shape)
    part_ref[:16] = select(dot(up_key_ref[...], got_ref[:, :kv], 1, 1), code, 16, 16)
    part_ref[16:] = select(dot(up_value_ref[...], got_ref[:, kv : 2 * kv], 1, 1), code, 16, 16)


def lora_kernel(code_ref, a_ref, b_ref, c_ref, d_ref, down_key_ref, down_value_ref, rows_ref, back_ref):
    code = code_ref[:1]
    total = (a_ref[...] + c_ref[...]) + (b_ref[...] + d_ref[...])
    back = (adapter_scale * total).astype(bf16)
    back_ref[...] = back
    rows = dot(spread(back[:16], code, 16), down_key_ref[...], 0, 0)
    rows = rows + dot(spread(back[16:], code, 16), down_value_ref[...], 0, 0)
    rows_ref[...] = rows.astype(bf16)


def low_kernel(code_ref, rows_ref, down_key_ref, down_value_ref, part_ref, kept_ref):
    kept_ref[...] = rows_ref[...]
    code = code_ref[:1]
    part_ref[:16] = select(dot(down_key_ref[...], rows_ref[...], 1, 1), code, 16, 16)
    part_ref[16:] = select(dot(down_value_ref[...], rows_ref[...], 1, 1), code, 16, 16)


def grads_kernel(code_ref, back_ref, a_ref, b_ref, c_ref, d_ref, rows_ref, got_ref,
                 down_key_out, down_value_out, up_key_out, up_value_out):
    code = code_ref[:1]
    kv = up_key_out.shape[1]
    low = ((a_ref[...] + c_ref[...]) + (b_ref[...] + d_ref[...])).astype(bf16)
    down_key_out[...] = dot(spread(back_ref[:16], code, 16), rows_ref[...], 1, 0)
    down_value_out[...] = dot(spread(back_ref[16:], code, 16), rows_ref[...], 1, 0)
    up_key_out[...] = adapter_scale * dot(spread(low[:16], code, 16), got_ref[:, :kv], 1, 0)
    up_value_out[...] = adapter_scale * dot(
        spread(low[16:], code, 16), got_ref[:, kv : 2 * kv], 1, 0
    )


def frozen_kernel(g0, g1, g2, g3, w0, w1, w2, w3, out_ref):
    total = dot(g0[...], w0[...], 1, 1)
    total = total + dot(g1[...], w1[...], 1, 1)
    total = total + dot(g2[...], w2[...], 1, 1)
    out_ref[...] = total + dot(g3[...], w3[...], 1, 1)


def final_kernel(route_ref, frozen_ref, rows_ref, out_ref, rows, frozen, total, result, sem):
    count, step = rows.shape[0], rows.shape[1]
    arrive = [
        pltpu.make_async_copy(rows_ref.at[pl.ds(i * step, step), :], rows.at[i], sem.at[i])
        for i in range(count)
    ]
    arrive.append(pltpu.make_async_copy(frozen_ref, frozen, sem.at[count]))
    for copy in arrive:
        copy.start()
    for i in range(count):
        arrive[i].wait()
        more = dot(route_ref[:, i * step : (i + 1) * step], rows[i], 1, 0)
        total[...] = more if i == 0 else total[...] + more
    arrive[count].wait()
    half = result.shape[1]
    leave = []
    for i in range(result.shape[0]):
        part = pl.ds(i * half, half)
        result[i] = (total[part, :] + frozen[part, :]).astype(bf16)
        leave.append(pltpu.make_async_copy(result.at[i], out_ref.at[part, :], sem.at[i]))
        leave[i].start()
    for copy in leave:
        copy.wait()


def final(route, frozen, rows, chunks):
    tokens, width = frozen.shape
    slots = rows.shape[0]
    return pl.pallas_call(
        final_kernel,
        out_shape=jax.ShapeDtypeStruct((tokens, width), bf16),
        in_specs=[
            pl.BlockSpec(memory_space=pltpu.VMEM),
            pl.BlockSpec(memory_space=pl.ANY),
            pl.BlockSpec(memory_space=pl.ANY),
        ],
        out_specs=pl.BlockSpec(memory_space=pltpu.HBM),
        scratch_shapes=[
            pltpu.VMEM((chunks, slots // chunks, width), bf16),
            pltpu.VMEM((tokens, width), f32),
            pltpu.VMEM((tokens, width), f32),
            pltpu.VMEM((2, tokens // 2, width), bf16),
            pltpu.SemaphoreType.DMA((chunks + 1,)),
        ],
        compiler_params=pltpu.CompilerParams(vmem_limit_bytes=48 * MIB),
        name="final",
    )(route, frozen, rows)


def hold_kernel(*refs):
    pass


def hold(x, after):
    return pl.pallas_call(
        hold_kernel,
        out_shape=jax.ShapeDtypeStruct(x.shape, x.dtype),
        in_specs=[pl.BlockSpec(memory_space=pltpu.HBM)]
        + [pl.BlockSpec(memory_space=pl.ANY)] * len(after),
        out_specs=pl.BlockSpec(memory_space=pltpu.HBM),
        input_output_aliases={0: 0},
        name="hold",
    )(x, *after)


def shift_tensor(x, s):
    return lax.ppermute(x, "tensor", [(i, (i + s) % 4) for i in range(4)])


def local(inputs, grad_key, grad_value, weight_key, weight_value, down_key, down_value,
          up_key, up_value, adapter_ids):
    tokens, width = inputs.shape
    kv = grad_key.shape[1]
    owners, rank = 64, down_key.shape[1]
    lr = down_key.shape[0] * rank
    slots = owners * SLOTS
    where = lax.axis_index("tensor").astype(jnp.int32).reshape(1)
    down_key, down_value = down_key.reshape(lr, width), down_value.reshape(lr, width)
    up_key, up_value = up_key.reshape(lr, kv), up_value.reshape(lr, kv)

    def weights(shifts, after):
        sliced = call(
            functools.partial(weights_kernel, shifts),
            [((width, 2 * kv), bf16)] * len(shifts), "weights", smem=1, staged=False,
            scratch=[pltpu.SemaphoreType.DMA((2 * len(shifts),))], after=after,
        )(where, weight_key, weight_value)
        return {s: shift_tensor(x, s) if s else x for s, x in zip(shifts, sliced)}

    target, sent = call(
        route_kernel, [((8, tokens), jnp.int32), ((slots, 2 * kv + 128), bf16)], "route"
    )(adapter_ids.reshape(1, tokens), grad_key, grad_value)
    got = lax.all_to_all(sent, "adapter", split_axis=0, concat_axis=0, tiled=True)
    placed, route = call(
        place_kernel, [((slots, width), bf16), ((tokens, slots), bf16)], "place"
    )(target, inputs)
    (both,) = call(join_kernel, [((tokens, 2 * kv), bf16)], "join", after=[target])(
        grad_key, grad_value
    )
    every = [both] + [shift_tensor(both, s) for s in (1, 2, 3)]
    placed = hold(placed, every[1:])
    held = lax.all_to_all(placed, "adapter", split_axis=0, concat_axis=0, tiled=True)
    part, code, got = call(
        back_kernel,
        [((2 * rank, slots), f32), ((8, slots), jnp.int32), ((slots, 2 * kv), bf16)], "back",
        loose=(0,),
    )(got, up_key, up_value)
    blocks = weights((1, 3), [part])
    sums = [part] + [shift_tensor(part, s) for s in (1, 2, 3)]
    rows, back = call(
        lora_kernel, [((slots, width), bf16), ((2 * rank, slots), bf16)], "lora"
    )(code, *sums, down_key, down_value)
    rows = hold(rows, [held, blocks[1], blocks[3]])
    returned = lax.all_to_all(rows, "adapter", split_axis=0, concat_axis=0, tiled=True)
    blocks |= weights((0, 2), [back])
    part, held = call(
        low_kernel, [((2 * rank, slots), f32), ((slots, width), bf16)], "low", loose=(1,)
    )(code, held, down_key, down_value)
    sums = [part] + [shift_tensor(part, s) for s in (1, 2, 3)]
    grads = call(
        grads_kernel, [((lr, width), f32)] * 2 + [((lr, kv), f32)] * 2, "grads"
    )(code, back, *sums, held, got)
    (frozen,) = call(
        frozen_kernel, [((tokens, width), f32)], "frozen", after=[grads[2]]
    )(*every, *[blocks[s] for s in range(4)])
    input_gradient = final(route, frozen, returned, 4)
    count = lr // rank
    return (
        input_gradient,
        grads[0].reshape(count, rank, width),
        grads[1].reshape(count, rank, width),
        grads[2].reshape(count, rank, kv),
        grads[3].reshape(count, rank, kv),
    )


def solution(mesh):
    wide = P("adapter", "tensor")
    frozen = P(None, "tensor")
    adapter = P("adapter", None, "tensor")
    return jax.shard_map(
        local,
        mesh=mesh,
        in_specs=(wide, wide, wide, frozen, frozen, adapter, adapter, adapter, adapter, P("adapter")),
        out_specs=(wide, adapter, adapter, adapter, adapter),
        check_vma=False,
    )
```

time: 208 us -> 199 us (0.957)
  Pallas kernels: 24.3 us -> 46.9 us
  starting transfers between devices: 52.3 us -> 40.8 us
  local copies, waits for them, and re-layouts: 20.1 us -> 8.63 us
  waiting for transfers between devices: 110 us -> 101 us
    all_to_all x1, waiting for transfers between devices: 28.8 us -> 2.23 us  [local(): lax.all_to_all(sent, 'adapter', split_axis=0, concat_axis=0, tiled=True)]
    pallas_call x12 -> x10, Pallas kernels: 24.3 us -> 42.4 us  [run(): pl.pallas_call(body, out_shape=[jax.ShapeDtypeStruct(s, d) for s, d in ou...]
    ppermute x12, starting transfers between devices: 29.1 us -> 15 us  [shift_tensor(): return lax.ppermute(x, 'tensor', [(i, (i + s) % 4) for i in range(4)])]
    unnamed x54 -> x32, local copies, waits for them, and re-layouts: 20.1 us -> 8.63 us
    ppermute x12, waiting for transfers between devices: 69.8 us -> 80.5 us  [shift_tensor(): return lax.ppermute(x, 'tensor', [(i, (i + s) % 4) for i in range(4)])]
    all_to_all x1, waiting for transfers between devices: 0.01 us -> 6.36 us  [local(): lax.all_to_all(rows, 'adapter', split_axis=0, concat_axis=0, tiled=True)]
    pallas_call x0 -> x3, Pallas kernels: none -> 4.48 us  [the longest x1 4.48 us: final(): pl.pallas_call(final_kernel, out_shape=jax.ShapeDtypeStruct((tokens, widt...]
    all_to_all x1, starting transfers between devices: 5.52 us -> 8.07 us  [local(): lax.all_to_all(placed, 'adapter', split_axis=0, concat_axis=0, tiled=True)]
  transfers between devices with their start and end apart: 15 -> 15, of which waited for: 7 -> 10; matrix products, arithmetic and copies ran while one was open for 0% -> 0% of each run, Pallas kernels for 9% -> 20%
where the time goes in v2:
time: 199 us; the launch traced here: 198 us
  waiting for transfers between devices  101 us (51%)
  Pallas kernels  46.9 us (24%)
  starting transfers between devices  40.8 us (21%)
  local copies, waits for them, and re-layouts  8.63 us (4%)
    ppermute x12, waiting for transfers between devices, shift_tensor(): return lax.ppermute(x, 'tensor', [(i, (i + s) % 4) for i in range(4)])  80.5 us
    pallas_call x10, Pallas kernels, run(): pl.pallas_call(body, out_shape=[jax.ShapeDtypeStruct(s, d) for s, d in ou...  42.4 us
    ppermute x12, starting transfers between devices, shift_tensor(): return lax.ppermute(x, 'tensor', [(i, (i + s) % 4) for i in range(4)])  15 us
    all_to_all x1, starting transfers between devices, local(): lax.all_to_all(sent, 'adapter', split_axis=0, concat_axis=0, tiled=True)  12.1 us
    all_to_all x1, waiting for transfers between devices, local(): lax.all_to_all(placed, 'adapter', split_axis=0, concat_axis=0, tiled=True)  11.7 us
    unnamed x32, local copies, waits for them, and re-layouts  8.63 us
    all_to_all x1, starting transfers between devices, local(): lax.all_to_all(placed, 'adapter', split_axis=0, concat_axis=0, tiled=True)  8.07 us
    all_to_all x1, waiting for transfers between devices, local(): lax.all_to_all(rows, 'adapter', split_axis=0, concat_axis=0, tiled=True)  6.36 us
  transfers between devices with their start and end apart: 15, of which 10 were waited for; matrix products, arithmetic and copies ran while one was open for 0% of the time, Pallas kernels for 20%

profile of v2, /device:TPU:8, one launch (start us, length us, event | category | flops | bytes accessed | tf_op | source)
XLA Modules:
  0.0 198.1 jit_solution(12066539373127520235)
XLA Ops:
  0.6 3.3 %route.1 = (s32[8,512]{1,0:T(8,128)}, bf16[1024,640]{1,0:T(8,128)(2,1)}) custom-call(s32[1,512]{1,0:T(1,128)} %bitcast.29, bf16[512,256]{1,0:T(8,128)(2,1)} %refs_0_.1, bf16[512,256]{1,0:T(8,128)(2,1)} %refs_1_.7), custom_call_target="tpu_custom_call" | custom-call | tf_op jit(solution)/shard_map/route/pallas_call | solution.py:51
  3.9 12.1 %all-to-all-start = ((bf16[64,16,640]{2,1,0:T(8,128)(2,1)}), bf16[64,16,640]{2,1,0:T(8,128)(2,1)S(1)}, u32[]{:S(2)}, u32[]{:S(2)}) async-start(bf16[64,16,640]{2,1,0:T(8,128)(2,1)} %bitcast.25), calls=%async_computation | async-start | bytes 2621440 | tf_op jit(solution)/shard_map/all_to_all | solution.py:274
  16.1 1.9 join.1.refs_0_
  18.0 2.8 %collective-permute-start.2 = (bf16[512,512]{1,0:T(8,128)(2,1)}, bf16[512,512]{1,0:T(8,128)(2,1)S(1)}, u32[]{:S(2)}, u32[]{:S(2)}) collective-permute-start(bf16[512,512]{1,0:T(8,128)(2,1)} %join.1.refs_0_), channel_id=1, source_target_pairs={{0,3},{1,0},{2,1},{3,2},{4,7},{5,4},{6,5},{7,6},{8,11},{9,8},{10,9... | collective-permute-start | bytes 1572872 | tf_op jit(solution)/shard_map/ppermute | solution.py:249
  20.8 0.8 collective-permute-start.1
  21.6 0.9 collective-permute-start
  22.5 4.8 %place.1 = (bf16[1024,1280]{1,0:T(8,128)(2,1)}, bf16[512,1024]{1,0:T(8,128)(2,1)}) custom-call(s32[8,512]{1,0:T(8,128)} %get-tuple-element.24.refs_0_.refs_2_, bf16[512,1280]{1,0:T(8,128)(2,1)} %refs_1_.6), custom_call_target="tpu_custom_call" | custom-call | tf_op jit(solution)/shard_map/place/pallas_call | solution.py:51
  27.3 16.6 %collective-permute-done.2.refs_3_ = bf16[512,512]{1,0:T(8,128)(2,1)S(1)} collective-permute-done((bf16[512,512]{1,0:T(8,128)(2,1)}, bf16[512,512]{1,0:T(8,128)(2,1)S(1)}, u32[]{:S(2)}, u32[]{:S(2)}) %collective-permute-start.2) | collective-permute-done | bytes 524320 | tf_op jit(solution)/shard_map/ppermute | solution.py:249
  43.9 0.0 collective-permute-done.1.refs_2_
  43.9 3.6 %collective-permute-done.refs_1_ = bf16[512,512]{1,0:T(8,128)(2,1)S(1)} collective-permute-done((bf16[512,512]{1,0:T(8,128)(2,1)}, bf16[512,512]{1,0:T(8,128)(2,1)S(1)}, u32[]{:S(2)}, u32[]{:S(2)}) %collective-permute-start) | collective-permute-done | bytes 524320 | tf_op jit(solution)/shard_map/ppermute | solution.py:249
  47.4 0.8 copy-done.7
  48.2 2.2 %all-to-all-done = bf16[64,16,640]{2,1,0:T(8,128)(2,1)S(1)} async-done(((bf16[64,16,640]{2,1,0:T(8,128)(2,1)}), bf16[64,16,640]{2,1,0:T(8,128)(2,1)S(1)}, u32[]{:S(2)}, u32[]{:S(2)}) %all-to-all-start) | async-done | bytes 1310752 | tf_op jit(solution)/shard_map/all_to_all | solution.py:274
  50.5 1.1 copy-done.4
  51.5 8.1 %all-to-all-start.1 = ((bf16[64,16,1280]{2,1,0:T(8,128)(2,1)}), bf16[64,16,1280]{2,1,0:T(8,128)(2,1)S(1)}, u32[]{:S(2)}, u32[]{:S(2)}) async-start(bf16[64,16,1280]{2,1,0:T(8,128)(2,1)} %bitcast.19), calls=%async_computation.1 | async-start | bytes 5242880 | tf_op jit(solution)/shard_map/all_to_all | solution.py:283
  59.6 3.0 %back.1 = (f32[32,1024]{1,0:T(8,128)}, s32[8,1024]{1,0:T(8,128)}, bf16[1024,512]{1,0:T(8,128)(2,1)}) custom-call(bf16[1024,640]{1,0:T(8,128)(2,1)} %bitcast.20, bf16[256,256]{1,0:T(8,128)(2,1)} %bitcast.27, bf16[256,256]{1,0:T(8,128)(2,1)} %bitcast.28), custom_call_target="tpu_custom_call" | custom-call | tf_op jit(solution)/shard_map/back/pallas_call | solution.py:51
  62.6 0.0 copy-start.9
  62.6 3.3 %weights.3 = (bf16[1280,512]{1,0:T(8,128)(2,1)}, bf16[1280,512]{1,0:T(8,128)(2,1)}) custom-call(s32[1]{0:T(128)} %bitcast.1.refs_0_, bf16[5120,256]{1,0:T(8,128)(2,1)} %refs_1_.9, bf16[5120,256]{1,0:T(8,128)(2,1)} %refs_2_.5, f32[32,1024]{1,0:T(8,128)} %get-tuple-element.28.refs_1_.refs_3_), custom_call_target="tpu_custom_call" | custom-call | tf_op jit(solution)/shard_map/weights/pallas_call | solution.py:51
  65.9 0.1 collective-permute-start.6
  65.9 3.2 %collective-permute-start.8 = (bf16[1280,512]{1,0:T(8,128)(2,1)}, bf16[1280,512]{1,0:T(8,128)(2,1)}, u32[]{:S(2)}, u32[]{:S(2)}) collective-permute-start(bf16[1280,512]{1,0:T(8,128)(2,1)} %get-tuple-element.33), channel_id=1, source_target_pairs={{0,3},{1,0},{2,1},{3,2},{4,7},{5,4},{6,5},{7,6},{8,11},{9,8},{10,9... | collective-permute-start | bytes 3932168 | tf_op jit(solution)/shard_map/ppermute | solution.py:249
  69.2 0.0 collective-permute-start.5
  69.2 0.9 collective-permute-start.4
  70.1 1.1 collective-permute-start.3
  71.2 31.9 %collective-permute-done.5.refs_4_ = f32[32,1024]{1,0:T(8,128)S(1)} collective-permute-done((f32[32,1024]{1,0:T(8,128)S(1)}, f32[32,1024]{1,0:T(8,128)S(1)}, u32[]{:S(2)}, u32[]{:S(2)}) %collective-permute-start.5) | collective-permute-done | bytes 131104 | tf_op jit(solution)/shard_map/ppermute | solution.py:249
  103.1 0.7 collective-permute-done.3.refs_2_
  103.8 0.6 copy-done.12
  104.5 4.8 %lora.1 = (bf16[1024,1280]{1,0:T(8,128)(2,1)}, bf16[32,1024]{1,0:T(8,128)(2,1)}) custom-call(s32[8,1024]{1,0:T(8,128)} %get-tuple-element.27.refs_0_, f32[32,1024]{1,0:T(8,128)} %get-tuple-element.28.refs_1_.refs_3_, f32[32,1024]{1,0:T(8,128)} %copy-done.12, f32[32,1024]{1,0:T(8,128)} %copy-done.11, f32[32,1024]{1,0:T(8,128)} %copy-done.10, ...), custom_call_target="tpu_custom_call" | custom-call | tf_op jit(solution)/shard_map/lora/pallas_call | solution.py:51
  109.3 0.0 collective-permute-done.6.refs_5_.refs_2_
  109.3 1.1 copy-done.3
  110.4 11.7 %all-to-all-done.1 = bf16[64,16,1280]{2,1,0:T(8,128)(2,1)S(1)} async-done(((bf16[64,16,1280]{2,1,0:T(8,128)(2,1)}), bf16[64,16,1280]{2,1,0:T(8,128)(2,1)S(1)}, u32[]{:S(2)}, u32[]{:S(2)}) %all-to-all-start.1) | async-done | bytes 2621472 | tf_op jit(solution)/shard_map/all_to_all | solution.py:283
  122.1 1.5 copy-done.2
  123.6 5.6 %all-to-all-start.2 = ((bf16[64,16,1280]{2,1,0:T(8,128)(2,1)}), bf16[64,16,1280]{2,1,0:T(8,128)(2,1)}, u32[]{:S(2)}, u32[]{:S(2)}) async-start(bf16[64,16,1280]{2,1,0:T(8,128)(2,1)} %bitcast.18), calls=%async_computation.2 | async-start | bytes 5242880 | tf_op jit(solution)/shard_map/all_to_all | solution.py:295
  129.2 3.2 %weights.2 = (bf16[1280,512]{1,0:T(8,128)(2,1)}, bf16[1280,512]{1,0:T(8,128)(2,1)}) custom-call(s32[1]{0:T(128)} %bitcast.1.refs_0_, bf16[5120,256]{1,0:T(8,128)(2,1)} %refs_1_.9, bf16[5120,256]{1,0:T(8,128)(2,1)} %refs_2_.5, bf16[32,1024]{1,0:T(8,128)(2,1)} %get-tuple-element.29.refs_3_.refs_1_), custom_call_target="tpu_custom_call" | custom-call | tf_op jit(solution)/shard_map/weights/pallas_call | solution.py:51
  132.5 0.9 collective-permute-start.7
  133.3 5.3 %low.1 = (f32[32,1024]{1,0:T(8,128)}, bf16[1024,1280]{1,0:T(8,128)(2,1)}) custom-call(s32[8,1024]{1,0:T(8,128)} %get-tuple-element.27.refs_0_, bf16[1024,1280]{1,0:T(8,128)(2,1)} %bitcast.17, bf16[256,1280]{1,0:T(8,128)(2,1)} %bitcast.22, bf16[256,1280]{1,0:T(8,128)(2,1)} %bitcast.24), custom_call_target="tpu_custom_call" | custom-call | tf_op jit(solution)/shard_map/low/pallas_call | solution.py:51
  138.6 1.3 collective-permute-start.11
  139.9 1.6 collective-permute-start.10
  141.6 1.3 collective-permute-start.9
  142.9 23.8 %collective-permute-done.11.refs_5_ = f32[32,1024]{1,0:T(8,128)S(1)} collective-permute-done((f32[32,1024]{1,0:T(8,128)}, f32[32,1024]{1,0:T(8,128)S(1)}, u32[]{:S(2)}, u32[]{:S(2)}) %collective-permute-start.11) | collective-permute-done | bytes 131104 | tf_op jit(solution)/shard_map/ppermute | solution.py:249
  166.7 2.1 %collective-permute-done.10.refs_4_ = f32[32,1024]{1,0:T(8,128)S(1)} collective-permute-done((f32[32,1024]{1,0:T(8,128)}, f32[32,1024]{1,0:T(8,128)S(1)}, u32[]{:S(2)}, u32[]{:S(2)}) %collective-permute-start.10) | collective-permute-done | bytes 131104 | tf_op jit(solution)/shard_map/ppermute | solution.py:249
  168.7 2.0 collective-permute-done.9.refs_3_
  170.7 0.6 copy-done.15
  171.4 5.1 %grads.1 = (f32[256,1280]{1,0:T(8,128)}, f32[256,1280]{1,0:T(8,128)}, f32[256,256]{1,0:T(8,128)}, f32[256,256]{1,0:T(8,128)}) custom-call(s32[8,1024]{1,0:T(8,128)} %get-tuple-element.27.refs_0_, bf16[32,1024]{1,0:T(8,128)(2,1)} %get-tuple-element.29.refs_3_.refs_1_, f32[32,1024]{1,0:T(8,128)} %get-tuple-element.35.refs_2_, f32[32,1024]{1,0:T(8,128)} %copy-done.15, ...), custom_call_target="tpu_custom_call" | custom-call | tf_op jit(solution)/shard_map/grads/pallas_call | solution.py:51
  176.5 0.0 collective-permute-done.7.refs_6_
  176.5 1.1 copy-done.8
  177.6 7.7 %frozen.1.frozen_ref = f32[512,1280]{1,0:T(8,128)} custom-call(bf16[512,512]{1,0:T(8,128)(2,1)} %join.1.refs_0_, bf16[512,512]{1,0:T(8,128)(2,1)} %copy-done.7, bf16[512,512]{1,0:T(8,128)(2,1)} %copy-done.6, bf16[512,512]{1,0:T(8,128)(2,1)} %copy-done.5, bf16[1280,512]{1,0:T(8,128)(2,1)} %get-tuple-element.30.refs_4_, bf16[1280,512]{1,0:T(8,128)(2,1)} %copy-done.3, ...), custom_call_target="tpu_custom_call" | custom-call | tf_op jit(solution)/shard_map/frozen/pallas_call | solution.py:51
  185.3 6.4 %all-to-all-done.2 = bf16[64,16,1280]{2,1,0:T(8,128)(2,1)} async-done(((bf16[64,16,1280]{2,1,0:T(8,128)(2,1)}), bf16[64,16,1280]{2,1,0:T(8,128)(2,1)}, u32[]{:S(2)}, u32[]{:S(2)}) %all-to-all-start.2) | async-done | bytes 2621472 | tf_op jit(solution)/shard_map/all_to_all | solution.py:295
  191.7 1.7 copy-done
  193.4 4.5 %final.1 = bf16[512,1280]{1,0:T(8,128)(2,1)} custom-call(bf16[512,1024]{1,0:T(8,128)(2,1)S(1)} %copy-done.1, f32[512,1280]{1,0:T(8,128)S(1)} %copy-done, bf16[1024,1280]{1,0:T(8,128)(2,1)} %bitcast.11.rows_ref), custom_call_target="tpu_custom_call" | custom-call | tf_op jit(solution)/shard_map/final/pallas_call | solution.py:211
  (27 shorter events, 0.0 us)
Async XLA Ops:
  3.9 46.5 %all-to-all-start = ((bf16[64,16,640]{2,1,0:T(8,128)(2,1)}), bf16[64,16,640]{2,1,0:T(8,128)(2,1)S(1)}, u32[]{:S(2)}, u32[]{:S(2)}) async-start(bf16[64,16,640]{2,1,0:T(8,128)(2,1)} %bitcast.25), calls=%async_computation | async-start | bytes 2621440 | tf_op jit(solution)/shard_map/all_to_all | solution.py:274
  18.0 25.9 %collective-permute-start.2 = (bf16[512,512]{1,0:T(8,128)(2,1)}, bf16[512,512]{1,0:T(8,128)(2,1)S(1)}, u32[]{:S(2)}, u32[]{:S(2)}) collective-permute-start(bf16[512,512]{1,0:T(8,128)(2,1)} %join.1.refs_0_), channel_id=1, source_target_pairs={{0,3},{1,0},{2,1},{3,2},{4,7},{5,4},{6,5},{7,6},{8,11},{9,8},{10,9... | collective-permute-start | bytes 1572872 | tf_op jit(solution)/shard_map/ppermute | solution.py:249
  20.8 23.1 %collective-permute-start.1 = (bf16[512,512]{1,0:T(8,128)(2,1)}, bf16[512,512]{1,0:T(8,128)(2,1)S(1)}, u32[]{:S(2)}, u32[]{:S(2)}) collective-permute-start(bf16[512,512]{1,0:T(8,128)(2,1)} %join.1.refs_0_), channel_id=1, source_target_pairs={{0,2},{1,3},{2,0},{3,1},{4,6},{5,7},{6,4},{7,5},{8,10},{9,11},{10,... | collective-permute-start | bytes 1572872 | tf_op jit(solution)/shard_map/ppermute | solution.py:249
  21.6 25.8 %collective-permute-start = (bf16[512,512]{1,0:T(8,128)(2,1)}, bf16[512,512]{1,0:T(8,128)(2,1)S(1)}, u32[]{:S(2)}, u32[]{:S(2)}) collective-permute-start(bf16[512,512]{1,0:T(8,128)(2,1)} %join.1.refs_0_), channel_id=1, source_target_pairs={{0,1},{1,2},{2,3},{3,0},{4,5},{5,6},{6,7},{7,4},{8,9},{9,10},{10,1... | collective-permute-start | bytes 1572872 | tf_op jit(solution)/shard_map/ppermute | solution.py:249
  43.9 3.6 %copy-start.5 = (bf16[512,512]{1,0:T(8,128)(2,1)}, bf16[512,512]{1,0:T(8,128)(2,1)S(1)}, u32[]{:S(2)}) copy-start(bf16[512,512]{1,0:T(8,128)(2,1)S(1)} %collective-permute-done.2.refs_3_) | copy-start | bytes 1572868
  43.9 3.6 %copy-start.6 = (bf16[512,512]{1,0:T(8,128)(2,1)}, bf16[512,512]{1,0:T(8,128)(2,1)S(1)}, u32[]{:S(2)}) copy-start(bf16[512,512]{1,0:T(8,128)(2,1)S(1)} %collective-permute-done.1.refs_2_) | copy-start | bytes 1572868
  47.4 0.8 copy-start.7
  50.5 1.1 copy-start.4
  51.5 70.6 %all-to-all-start.1 = ((bf16[64,16,1280]{2,1,0:T(8,128)(2,1)}), bf16[64,16,1280]{2,1,0:T(8,128)(2,1)S(1)}, u32[]{:S(2)}, u32[]{:S(2)}) async-start(bf16[64,16,1280]{2,1,0:T(8,128)(2,1)} %bitcast.19), calls=%async_computation.1 | async-start | bytes 5242880 | tf_op jit(solution)/shard_map/all_to_all | solution.py:283
  62.6 6.6 %copy-start.9 = (f32[32,1024]{1,0:T(8,128)S(1)}, f32[32,1024]{1,0:T(8,128)}, u32[]{:S(2)}) copy-start(f32[32,1024]{1,0:T(8,128)} %get-tuple-element.28.refs_1_.refs_3_) | copy-start | bytes 393220
  65.9 43.4 %collective-permute-start.6 = (bf16[1280,512]{1,0:T(8,128)(2,1)}, bf16[1280,512]{1,0:T(8,128)(2,1)S(1)}, u32[]{:S(2)}, u32[]{:S(2)}) collective-permute-start(bf16[1280,512]{1,0:T(8,128)(2,1)} %get-tuple-element.31), channel_id=1, source_target_pairs={{0,1},{1,2},{2,3},{3,0},{4,5},{5,6},{6,7},{7,4},{8,9},{9,10},{10,1... | collective-permute-start | bytes 3932168 | tf_op jit(solution)/shard_map/ppermute | solution.py:249
  65.9 44.5 %collective-permute-start.8 = (bf16[1280,512]{1,0:T(8,128)(2,1)}, bf16[1280,512]{1,0:T(8,128)(2,1)}, u32[]{:S(2)}, u32[]{:S(2)}) collective-permute-start(bf16[1280,512]{1,0:T(8,128)(2,1)} %get-tuple-element.33), channel_id=1, source_target_pairs={{0,3},{1,0},{2,1},{3,2},{4,7},{5,4},{6,5},{7,6},{8,11},{9,8},{10,9... | collective-permute-start | bytes 3932168 | tf_op jit(solution)/shard_map/ppermute | solution.py:249
  69.2 33.9 %collective-permute-start.5 = (f32[32,1024]{1,0:T(8,128)S(1)}, f32[32,1024]{1,0:T(8,128)S(1)}, u32[]{:S(2)}, u32[]{:S(2)}) collective-permute-start(f32[32,1024]{1,0:T(8,128)S(1)} %copy-done.9), channel_id=1, source_target_pairs={{0,3},{1,0},{2,1},{3,2},{4,7},{5,4},{6,5},{7,6},{8,11},{9,8},{10,9... | collective-permute-start | bytes 393224 | tf_op jit(solution)/shard_map/ppermute | solution.py:249
  69.2 33.9 %collective-permute-start.4 = (f32[32,1024]{1,0:T(8,128)S(1)}, f32[32,1024]{1,0:T(8,128)S(1)}, u32[]{:S(2)}, u32[]{:S(2)}) collective-permute-start(f32[32,1024]{1,0:T(8,128)S(1)} %copy-done.9), channel_id=1, source_target_pairs={{0,2},{1,3},{2,0},{3,1},{4,6},{5,7},{6,4},{7,5},{8,10},{9,11},{10,... | collective-permute-start | bytes 393224 | tf_op jit(solution)/shard_map/ppermute | solution.py:249
  70.1 33.7 %collective-permute-start.3 = (f32[32,1024]{1,0:T(8,128)S(1)}, f32[32,1024]{1,0:T(8,128)S(1)}, u32[]{:S(2)}, u32[]{:S(2)}) collective-permute-start(f32[32,1024]{1,0:T(8,128)S(1)} %copy-done.9), channel_id=1, source_target_pairs={{0,1},{1,2},{2,3},{3,0},{4,5},{5,6},{6,7},{7,4},{8,9},{9,10},{10,1... | collective-permute-start | bytes 393224 | tf_op jit(solution)/shard_map/ppermute | solution.py:249
  103.1 0.7 copy-start.10
  103.1 0.7 copy-start.11
  103.8 0.7 copy-start.12
  109.3 1.1 copy-start.3
  122.1 1.5 copy-start.2
  123.6 68.1 %all-to-all-start.2 = ((bf16[64,16,1280]{2,1,0:T(8,128)(2,1)}), bf16[64,16,1280]{2,1,0:T(8,128)(2,1)}, u32[]{:S(2)}, u32[]{:S(2)}) async-start(bf16[64,16,1280]{2,1,0:T(8,128)(2,1)} %bitcast.18), calls=%async_computation.2 | async-start | bytes 5242880 | tf_op jit(solution)/shard_map/all_to_all | solution.py:295
  132.5 44.1 %collective-permute-start.7 = (bf16[1280,512]{1,0:T(8,128)(2,1)}, bf16[1280,512]{1,0:T(8,128)(2,1)S(1)}, u32[]{:S(2)}, u32[]{:S(2)}) collective-permute-start(bf16[1280,512]{1,0:T(8,128)(2,1)} %get-tuple-element.32), channel_id=1, source_target_pairs={{0,2},{1,3},{2,0},{3,1},{4,6},{5,7},{6,4},{7,5},{8,10},{9,11},{10,... | collective-permute-start | bytes 3932168 | tf_op jit(solution)/shard_map/ppermute | solution.py:249
  138.6 28.0 %collective-permute-start.11 = (f32[32,1024]{1,0:T(8,128)}, f32[32,1024]{1,0:T(8,128)S(1)}, u32[]{:S(2)}, u32[]{:S(2)}) collective-permute-start(f32[32,1024]{1,0:T(8,128)} %get-tuple-element.35.refs_2_), channel_id=1, source_target_pairs={{0,3},{1,0},{2,1},{3,2},{4,7},{5,4},{6,5},{7,6},{8,11},{9,8},{10,9... | collective-permute-start | bytes 393224 | tf_op jit(solution)/shard_map/ppermute | solution.py:249
  139.9 28.8 %collective-permute-start.10 = (f32[32,1024]{1,0:T(8,128)}, f32[32,1024]{1,0:T(8,128)S(1)}, u32[]{:S(2)}, u32[]{:S(2)}) collective-permute-start(f32[32,1024]{1,0:T(8,128)} %get-tuple-element.35.refs_2_), channel_id=1, source_target_pairs={{0,2},{1,3},{2,0},{3,1},{4,6},{5,7},{6,4},{7,5},{8,10},{9,11},{10,... | collective-permute-start | bytes 393224 | tf_op jit(solution)/shard_map/ppermute | solution.py:249
  141.6 29.1 %collective-permute-start.9 = (f32[32,1024]{1,0:T(8,128)}, f32[32,1024]{1,0:T(8,128)S(1)}, u32[]{:S(2)}, u32[]{:S(2)}) collective-permute-start(f32[32,1024]{1,0:T(8,128)} %get-tuple-element.35.refs_2_), channel_id=1, source_target_pairs={{0,1},{1,2},{2,3},{3,0},{4,5},{5,6},{6,7},{7,4},{8,9},{9,10},{10,1... | collective-permute-start | bytes 393224 | tf_op jit(solution)/shard_map/ppermute | solution.py:249
  166.7 4.0 %copy-start.13 = (f32[32,1024]{1,0:T(8,128)}, f32[32,1024]{1,0:T(8,128)S(1)}, u32[]{:S(2)}) copy-start(f32[32,1024]{1,0:T(8,128)S(1)} %collective-permute-done.11.refs_5_) | copy-start | bytes 393220
  168.7 2.0 %copy-start.14 = (f32[32,1024]{1,0:T(8,128)}, f32[32,1024]{1,0:T(8,128)S(1)}, u32[]{:S(2)}) copy-start(f32[32,1024]{1,0:T(8,128)S(1)} %collective-permute-done.10.refs_4_) | copy-start | bytes 393220
  170.7 0.7 copy-start.15
  176.5 1.1 copy-start.8
  177.6 14.1 %copy-start.1 = (bf16[512,1024]{1,0:T(8,128)(2,1)S(1)}, bf16[512,1024]{1,0:T(8,128)(2,1)}, u32[]{:S(2)}) copy-start(bf16[512,1024]{1,0:T(8,128)(2,1)} %get-tuple-element.25.route_ref) | copy-start | bytes 3145732
  191.7 1.7 copy-start

commit v3 on v2

--- a/solution.py
+++ b/solution.py
@@ -23,12 +23,12 @@
         copy.wait()
 
 
-def call(kernel, outs, name, vmem=56, smem=0, scratch=(), after=(), staged=True, loose=()):
+def call(kernel, outs, name, vmem=63, smem=0, scratch=(), after=(), staged=True):
     def run(*args):
         count, first = len(args), len(args) + len(after)
         specs = [
             pl.BlockSpec(
-                memory_space=pltpu.SMEM if i < smem else pl.ANY if i in loose else pltpu.HBM
+                memory_space=pltpu.SMEM if i < smem else pltpu.HBM
             )
             for i in range(count)
         ]
@@ -68,7 +68,7 @@
 def route_kernel(ids_ref, key_ref, value_ref, target_ref, sent_ref):
     ids = ids_ref[...]
     tokens = ids.shape[1]
-    slots = sent_ref.shape[0]
+    slots = 2 * sent_ref.shape[0]
     owner = ids >> 4
     within = ids & 15
     owner_hot = lax.broadcasted_iota(jnp.int32, (slots // SLOTS, tokens), 0) == owner
@@ -77,14 +77,31 @@
     )
     before = dot(owner_hot.astype(f32).astype(bf16), earlier.astype(f32).astype(bf16), 1, 0)
     rank = jnp.sum(jnp.where(owner_hot, before, 0.0), axis=0, keepdims=True).astype(jnp.int32)
-    target = owner * SLOTS + rank
+    target = (rank >> 3) * (slots // 2) + owner * (SLOTS // 2) + (rank & 7)
     target_ref[...] = jnp.broadcast_to(target, target_ref.shape)
     route = routing(target, slots)
     kv = key_ref.shape[1]
-    sent_ref[:, :kv] = dot(route, key_ref[...], 1, 0).astype(bf16)
-    sent_ref[:, kv : 2 * kv] = dot(route, value_ref[...], 1, 0).astype(bf16)
     code = jnp.broadcast_to((within + 1).astype(f32), (128, tokens)).astype(bf16)
-    sent_ref[:, 2 * kv :] = dot(route, code, 1, 1).astype(bf16)
+    key = dot(route, key_ref[...], 1, 0).astype(bf16)
+    value = dot(route, value_ref[...], 1, 0).astype(bf16)
+    code = dot(route, code, 1, 1)
+    half = slots // 2
+    for h in range(2):
+        rows = slice(h * half, (h + 1) * half)
+        sent_ref[:, 2 * h * kv : (2 * h + 1) * kv] = key[rows]
+        sent_ref[:, (2 * h + 1) * kv : (2 * h + 2) * kv] = value[rows]
+    lane = lax.broadcasted_iota(jnp.int32, (half, 128), 1)
+    sent_ref[:, 4 * kv :] = jnp.where(lane == 0, code[:half], code[half:]).astype(bf16)
+
+
+def beside(rows):
+    half = rows.shape[0] // 2
+    return jnp.concatenate([rows[:half], rows[half:]], axis=1)
+
+
+def below(rows):
+    half = rows.shape[1] // 2
+    return jnp.concatenate([rows[:, :half], rows[:, half:]], axis=0)
 
 
 def routing(target, slots):
@@ -93,8 +110,8 @@
 
 
 def place_kernel(target_ref, inputs_ref, out_ref, back_ref):
-    route = routing(target_ref[:1], out_ref.shape[0])
-    out_ref[...] = dot(route, inputs_ref[...], 1, 0).astype(bf16)
+    route = routing(target_ref[:1], 2 * out_ref.shape[0])
+    out_ref[...] = beside(dot(route, inputs_ref[...], 1, 0).astype(bf16))
     back_ref[...] = route.T
 
 
@@ -116,8 +133,11 @@
 
 
 def code_row(meta):
-    pick = (lax.broadcasted_iota(jnp.int32, (8, 128), 1) == 0).astype(f32).astype(bf16)
-    return dot(pick, meta, 1, 1)[:1].astype(jnp.int32)
+    pick = lax.broadcasted_iota(jnp.int32, (8, 128), 0) == lax.broadcasted_iota(
+        jnp.int32, (8, 128), 1
+    )
+    code = dot(pick.astype(f32).astype(bf16), meta, 1, 1).astype(jnp.int32)
+    return jnp.concatenate([code[:1], code[1:2]], axis=1)
 
 
 def select(expanded, code, count, rank):
@@ -136,11 +156,11 @@
 
 def back_kernel(got_ref, up_key_ref, up_value_ref, part_ref, code_ref, kept_ref):
     kv = up_key_ref.shape[1]
-    kept_ref[...] = got_ref[:, : 2 * kv]
-    code = code_row(got_ref[:, 2 * kv :])
+    kept_ref[...] = below(got_ref[:, : 4 * kv])
+    code = code_row(got_ref[:, 4 * kv :])
     code_ref[...] = jnp.broadcast_to(code, code_ref.shape)
-    part_ref[:16] = select(dot(up_key_ref[...], got_ref[:, :kv], 1, 1), code, 16, 16)
-    part_ref[16:] = select(dot(up_value_ref[...], got_ref[:, kv : 2 * kv], 1, 1), code, 16, 16)
+    part_ref[:16] = select(dot(up_key_ref[...], kept_ref[:, :kv], 1, 1), code, 16, 16)
+    part_ref[16:] = select(dot(up_value_ref[...], kept_ref[:, kv:], 1, 1), code, 16, 16)
 
 
 def lora_kernel(code_ref, a_ref, b_ref, c_ref, d_ref, down_key_ref, down_value_ref, rows_ref, back_ref):
@@ -150,14 +170,14 @@
     back_ref[...] = back
     rows = dot(spread(back[:16], code, 16), down_key_ref[...], 0, 0)
     rows = rows + dot(spread(back[16:], code, 16), down_value_ref[...], 0, 0)
-    rows_ref[...] = rows.astype(bf16)
+    rows_ref[...] = beside(rows.astype(bf16))
 
 
 def low_kernel(code_ref, rows_ref, down_key_ref, down_value_ref, part_ref, kept_ref):
-    kept_ref[...] = rows_ref[...]
+    kept_ref[...] = below(rows_ref[...])
     code = code_ref[:1]
-    part_ref[:16] = select(dot(down_key_ref[...], rows_ref[...], 1, 1), code, 16, 16)
-    part_ref[16:] = select(dot(down_value_ref[...], rows_ref[...], 1, 1), code, 16, 16)
+    part_ref[:16] = select(dot(down_key_ref[...], kept_ref[...], 1, 1), code, 16, 16)
+    part_ref[16:] = select(dot(down_value_ref[...], kept_ref[...], 1, 1), code, 16, 16)
 
 
 def grads_kernel(code_ref, back_ref, a_ref, b_ref, c_ref, d_ref, rows_ref, got_ref,
@@ -180,51 +200,49 @@
     out_ref[...] = total + dot(g3[...], w3[...], 1, 1)
 
 
-def final_kernel(route_ref, frozen_ref, rows_ref, out_ref, rows, frozen, total, result, sem):
-    count, step = rows.shape[0], rows.shape[1]
+def final_kernel(columns, route_ref, frozen_ref, rows_ref, out_ref, route, frozen, rows, result, sem, sem_out):
+    half, width = rows.shape[0], frozen.shape[1]
     arrive = [
-        pltpu.make_async_copy(rows_ref.at[pl.ds(i * step, step), :], rows.at[i], sem.at[i])
-        for i in range(count)
+        pltpu.make_async_copy(a, b, sem.at[i])
+        for i, (a, b) in enumerate([(route_ref, route), (rows_ref, rows), (frozen_ref, frozen)])
     ]
-    arrive.append(pltpu.make_async_copy(frozen_ref, frozen, sem.at[count]))
+    leave = []
     for copy in arrive:
         copy.start()
-    for i in range(count):
-        arrive[i].wait()
-        more = dot(route_ref[:, i * step : (i + 1) * step], rows[i], 1, 0)
-        total[...] = more if i == 0 else total[...] + more
-    arrive[count].wait()
-    half = result.shape[1]
-    leave = []
+    arrive[0].wait()
+    arrive[1].wait()
     for i in range(result.shape[0]):
-        part = pl.ds(i * half, half)
-        result[i] = (total[part, :] + frozen[part, :]).astype(bf16)
-        leave.append(pltpu.make_async_copy(result.at[i], out_ref.at[part, :], sem.at[i]))
+        at = i * columns
+        total = dot(route[:, :half], rows[:, at : at + columns], 1, 0)
+        total = total + dot(route[:, half:], rows[:, width + at : width + at + columns], 1, 0)
+        if i == 0:
+            arrive[2].wait()
+        result[i] = (total + frozen[:, at : at + columns]).astype(bf16)
+        leave.append(
+            pltpu.make_async_copy(result.at[i], out_ref.at[:, pl.ds(at, columns)], sem_out.at[i])
+        )
         leave[i].start()
     for copy in leave:
         copy.wait()
 
 
-def final(route, frozen, rows, chunks):
+def final(route, frozen, rows, columns):
     tokens, width = frozen.shape
-    slots = rows.shape[0]
+    count = width // columns
     return pl.pallas_call(
-        final_kernel,
+        functools.partial(final_kernel, columns),
         out_shape=jax.ShapeDtypeStruct((tokens, width), bf16),
-        in_specs=[
-            pl.BlockSpec(memory_space=pltpu.VMEM),
-            pl.BlockSpec(memory_space=pl.ANY),
-            pl.BlockSpec(memory_space=pl.ANY),
-        ],
+        in_specs=[pl.BlockSpec(memory_space=pltpu.HBM)] * 3,
         out_specs=pl.BlockSpec(memory_space=pltpu.HBM),
         scratch_shapes=[
-            pltpu.VMEM((chunks, slots // chunks, width), bf16),
-            pltpu.VMEM((tokens, width), f32),
-            pltpu.VMEM((tokens, width), f32),
-            pltpu.VMEM((2, tokens // 2, width), bf16),
-            pltpu.SemaphoreType.DMA((chunks + 1,)),
+            pltpu.VMEM(route.shape, bf16),
+            pltpu.VMEM(frozen.shape, f32),
+            pltpu.VMEM(rows.shape, bf16),
+            pltpu.VMEM((count, tokens, columns), bf16),
+            pltpu.SemaphoreType.DMA((3,)),
+            pltpu.SemaphoreType.DMA((count,)),
         ],
-        compiler_params=pltpu.CompilerParams(vmem_limit_bytes=48 * MIB),
+        compiler_params=pltpu.CompilerParams(vmem_limit_bytes=63 * MIB),
         name="final",
     )(route, frozen, rows)
 
@@ -269,33 +287,32 @@
         return {s: shift_tensor(x, s) if s else x for s, x in zip(shifts, sliced)}
 
     target, sent = call(
-        route_kernel, [((8, tokens), jnp.int32), ((slots, 2 * kv + 128), bf16)], "route"
+        route_kernel, [((8, tokens), jnp.int32), ((slots // 2, 4 * kv + 128), bf16)], "route"
     )(adapter_ids.reshape(1, tokens), grad_key, grad_value)
     got = lax.all_to_all(sent, "adapter", split_axis=0, concat_axis=0, tiled=True)
     placed, route = call(
-        place_kernel, [((slots, width), bf16), ((tokens, slots), bf16)], "place"
+        place_kernel, [((slots // 2, 2 * width), bf16), ((tokens, slots), bf16)], "place"
     )(target, inputs)
     (both,) = call(join_kernel, [((tokens, 2 * kv), bf16)], "join", after=[target])(
         grad_key, grad_value
     )
     every = [both] + [shift_tensor(both, s) for s in (1, 2, 3)]
-    placed = hold(placed, every[1:])
+    placed = hold(placed, [every[1], every[3]])
     held = lax.all_to_all(placed, "adapter", split_axis=0, concat_axis=0, tiled=True)
     part, code, got = call(
         back_kernel,
         [((2 * rank, slots), f32), ((8, slots), jnp.int32), ((slots, 2 * kv), bf16)], "back",
-        loose=(0,),
     )(got, up_key, up_value)
     blocks = weights((1, 3), [part])
     sums = [part] + [shift_tensor(part, s) for s in (1, 2, 3)]
     rows, back = call(
-        lora_kernel, [((slots, width), bf16), ((2 * rank, slots), bf16)], "lora"
+        lora_kernel, [((slots // 2, 2 * width), bf16), ((2 * rank, slots), bf16)], "lora"
     )(code, *sums, down_key, down_value)
-    rows = hold(rows, [held, blocks[1], blocks[3]])
+    rows = hold(rows, [held, blocks[1], blocks[3], every[2]])
     returned = lax.all_to_all(rows, "adapter", split_axis=0, concat_axis=0, tiled=True)
     blocks |= weights((0, 2), [back])
     part, held = call(
-        low_kernel, [((2 * rank, slots), f32), ((slots, width), bf16)], "low", loose=(1,)
+        low_kernel, [((2 * rank, slots), f32), ((slots, width), bf16)], "low"
     )(code, held, down_key, down_value)
     sums = [part] + [shift_tensor(part, s) for s in (1, 2, 3)]
     grads = call(
@@ -304,7 +321,7 @@
     (frozen,) = call(
         frozen_kernel, [((tokens, width), f32)], "frozen", after=[grads[2]]
     )(*every, *[blocks[s] for s in range(4)])
-    input_gradient = final(route, frozen, returned, 4)
+    input_gradient = final(route, frozen, returned, 256)
     count = lr // rank
     return (
         input_gradient,

time: 199 us -> 199 us (level)
  local copies, waits for them, and re-layouts: 8.63 us -> 1.33 us
  waiting for transfers between devices: 101 us -> 105 us
  starting transfers between devices: 40.8 us -> 44.3 us
    all_to_all x1, waiting for transfers between devices: 11.7 us -> 0.01 us  [local(): lax.all_to_all(placed, 'adapter', split_axis=0, concat_axis=0, tiled=True)]
    all_to_all x1, waiting for transfers between devices: 2.23 us -> 11.6 us  [local(): lax.all_to_all(sent, 'adapter', split_axis=0, concat_axis=0, tiled=True)]
    unnamed x32 -> x18, local copies, waits for them, and re-layouts: 8.63 us -> 1.33 us
    ppermute x12, waiting for transfers between devices: 80.5 us -> 85.6 us  [shift_tensor(): return lax.ppermute(x, 'tensor', [(i, (i + s) % 4) for i in range(4)])]
    all_to_all x1, starting transfers between devices: 5.6 us -> 10.5 us  [local(): lax.all_to_all(rows, 'adapter', split_axis=0, concat_axis=0, tiled=True)]
    all_to_all x1, starting transfers between devices: 8.07 us -> 5.79 us  [local(): lax.all_to_all(placed, 'adapter', split_axis=0, concat_axis=0, tiled=True)]
  transfers between devices with their start and end apart: 15 -> 15, of which waited for: 10 -> 9; matrix products, arithmetic and copies ran while one was open for 0% -> 0% of each run, Pallas kernels for 20% -> 20%
where the time goes in v3:
time: 199 us; the launch traced here: 198 us
  waiting for transfers between devices  105 us (53%)
  Pallas kernels  47.1 us (24%)
  starting transfers between devices  44.3 us (22%)
    ppermute x12, waiting for transfers between devices, shift_tensor(): return lax.ppermute(x, 'tensor', [(i, (i + s) % 4) for i in range(4)])  85.6 us
    pallas_call x10, Pallas kernels, run(): pl.pallas_call(body, out_shape=[jax.ShapeDtypeStruct(s, d) for s, d in ou...  42.1 us
    ppermute x12, starting transfers between devices, shift_tensor(): return lax.ppermute(x, 'tensor', [(i, (i + s) % 4) for i in range(4)])  15.7 us
    all_to_all x1, starting transfers between devices, local(): lax.all_to_all(sent, 'adapter', split_axis=0, concat_axis=0, tiled=True)  12.3 us
    all_to_all x1, waiting for transfers between devices, local(): lax.all_to_all(sent, 'adapter', split_axis=0, concat_axis=0, tiled=True)  11.6 us
    all_to_all x1, starting transfers between devices, local(): lax.all_to_all(rows, 'adapter', split_axis=0, concat_axis=0, tiled=True)  10.5 us
    all_to_all x1, waiting for transfers between devices, local(): lax.all_to_all(rows, 'adapter', split_axis=0, concat_axis=0, tiled=True)  7.47 us
    all_to_all x1, starting transfers between devices, local(): lax.all_to_all(placed, 'adapter', split_axis=0, concat_axis=0, tiled=True)  5.79 us
  transfers between devices with their start and end apart: 15, of which 9 were waited for; matrix products, arithmetic and copies ran while one was open for 0% of the time, Pallas kernels for 20%

profile of v3, /device:TPU:8, one launch (start us, length us, event | category | flops | bytes accessed | tf_op | source)
XLA Modules:
  0.0 198.4 jit_solution(7651632101113059361)
XLA Ops:
  0.6 3.2 %route.1 = (s32[8,512]{1,0:T(8,128)}, bf16[512,1152]{1,0:T(8,128)(2,1)}) custom-call(s32[1,512]{1,0:T(1,128)} %bitcast.26, bf16[512,256]{1,0:T(8,128)(2,1)} %refs_0_.1, bf16[512,256]{1,0:T(8,128)(2,1)} %refs_1_.7), custom_call_target="tpu_custom_call" | custom-call | tf_op jit(solution)/shard_map/route/pallas_call | solution.py:51
  3.9 12.3 %all-to-all-start = ((bf16[64,8,1152]{2,1,0:T(8,128)(2,1)}), bf16[64,8,1152]{2,1,0:T(8,128)(2,1)}, u32[]{:S(2)}, u32[]{:S(2)}) async-start(bf16[64,8,1152]{2,1,0:T(8,128)(2,1)} %bitcast.22), calls=%async_computation | async-start | bytes 2359296 | tf_op jit(solution)/shard_map/all_to_all | solution.py:292
  16.2 1.9 join.1.refs_0_
  18.1 2.8 %collective-permute-start.2 = (bf16[512,512]{1,0:T(8,128)(2,1)}, bf16[512,512]{1,0:T(8,128)(2,1)S(1)}, u32[]{:S(2)}, u32[]{:S(2)}) collective-permute-start(bf16[512,512]{1,0:T(8,128)(2,1)} %join.1.refs_0_), channel_id=1, source_target_pairs={{0,3},{1,0},{2,1},{3,2},{4,7},{5,4},{6,5},{7,6},{8,11},{9,8},{10,9... | collective-permute-start | bytes 1572872 | tf_op jit(solution)/shard_map/ppermute | solution.py:267
  20.9 0.0 collective-permute-start
  20.9 4.8 %place.1 = (bf16[512,2560]{1,0:T(8,128)(2,1)}, bf16[512,1024]{1,0:T(8,128)(2,1)}) custom-call(s32[8,512]{1,0:T(8,128)} %get-tuple-element.24.refs_0_.refs_2_, bf16[512,1280]{1,0:T(8,128)(2,1)} %refs_1_.6), custom_call_target="tpu_custom_call" | custom-call | tf_op jit(solution)/shard_map/place/pallas_call | solution.py:51
  25.7 7.1 %collective-permute-done.2.refs_2_.refs_3_ = bf16[512,512]{1,0:T(8,128)(2,1)S(1)} collective-permute-done((bf16[512,512]{1,0:T(8,128)(2,1)}, bf16[512,512]{1,0:T(8,128)(2,1)S(1)}, u32[]{:S(2)}, u32[]{:S(2)}) %collective-permute-start.2) | collective-permute-done | bytes 524320 | tf_op jit(solution)/shard_map/ppermute | solution.py:267
  32.7 3.4 %collective-permute-done.refs_1_ = bf16[512,512]{1,0:T(8,128)(2,1)} collective-permute-done((bf16[512,512]{1,0:T(8,128)(2,1)}, bf16[512,512]{1,0:T(8,128)(2,1)}, u32[]{:S(2)}, u32[]{:S(2)}) %collective-permute-start) | collective-permute-done | bytes 524320 | tf_op jit(solution)/shard_map/ppermute | solution.py:267
  36.1 0.0 copy-done
  36.1 11.6 %all-to-all-done = bf16[64,8,1152]{2,1,0:T(8,128)(2,1)} async-done(((bf16[64,8,1152]{2,1,0:T(8,128)(2,1)}), bf16[64,8,1152]{2,1,0:T(8,128)(2,1)}, u32[]{:S(2)}, u32[]{:S(2)}) %all-to-all-start) | async-done | bytes 1179680 | tf_op jit(solution)/shard_map/all_to_all | solution.py:292
  47.7 5.8 %all-to-all-start.1 = ((bf16[64,8,2560]{2,1,0:T(8,128)(2,1)}), bf16[64,8,2560]{2,1,0:T(8,128)(2,1)}, u32[]{:S(2)}, u32[]{:S(2)}) async-start(bf16[64,8,2560]{2,1,0:T(8,128)(2,1)} %bitcast.16), calls=%async_computation.1 | async-start | bytes 5242880 | tf_op jit(solution)/shard_map/all_to_all | solution.py:301
  53.5 2.9 %back.1 = (f32[32,1024]{1,0:T(8,128)}, s32[8,1024]{1,0:T(8,128)}, bf16[1024,512]{1,0:T(8,128)(2,1)}) custom-call(bf16[512,1152]{1,0:T(8,128)(2,1)} %bitcast.3.refs_0_, bf16[256,256]{1,0:T(8,128)(2,1)} %bitcast.24, bf16[256,256]{1,0:T(8,128)(2,1)} %bitcast.25), custom_call_target="tpu_custom_call" | custom-call | tf_op jit(solution)/shard_map/back/pallas_call | solution.py:51
  56.4 0.0 copy-start.1
  56.4 0.0 copy-start.2
  56.4 3.3 %weights.3 = (bf16[1280,512]{1,0:T(8,128)(2,1)}, bf16[1280,512]{1,0:T(8,128)(2,1)}) custom-call(s32[1]{0:T(128)} %bitcast.1.refs_0_, bf16[5120,256]{1,0:T(8,128)(2,1)} %refs_1_.9, bf16[5120,256]{1,0:T(8,128)(2,1)} %refs_2_.5, f32[32,1024]{1,0:T(8,128)} %get-tuple-element.28.refs_1_.refs_3_), custom_call_target="tpu_custom_call" | custom-call | tf_op jit(solution)/shard_map/weights/pallas_call | solution.py:51
  59.7 1.6 collective-permute-start.6
  61.3 1.7 collective-permute-start.8
  63.1 1.8 collective-permute-start.1
  64.9 1.1 collective-permute-start.5
  66.0 1.5 collective-permute-start.4
  67.5 40.7 %collective-permute-done.5.refs_4_ = f32[32,1024]{1,0:T(8,128)S(1)} collective-permute-done((f32[32,1024]{1,0:T(8,128)S(1)}, f32[32,1024]{1,0:T(8,128)S(1)}, u32[]{:S(2)}, u32[]{:S(2)}) %collective-permute-start.5) | collective-permute-done | bytes 131104 | tf_op jit(solution)/shard_map/ppermute | solution.py:267
  108.2 0.0 collective-permute-start.3
  108.2 0.0 collective-permute-done.4.refs_3_
  108.2 0.0 copy-start.4
  108.2 6.6 %collective-permute-done.3.refs_2_ = f32[32,1024]{1,0:T(8,128)S(1)} collective-permute-done((f32[32,1024]{1,0:T(8,128)S(1)}, f32[32,1024]{1,0:T(8,128)S(1)}, u32[]{:S(2)}, u32[]{:S(2)}) %collective-permute-start.3) | collective-permute-done | bytes 131104 | tf_op jit(solution)/shard_map/ppermute | solution.py:267
  114.8 0.7 copy-done.5
  115.5 4.8 %lora.1 = (bf16[512,2560]{1,0:T(8,128)(2,1)}, bf16[32,1024]{1,0:T(8,128)(2,1)}) custom-call(s32[8,1024]{1,0:T(8,128)} %get-tuple-element.27.refs_0_, f32[32,1024]{1,0:T(8,128)} %get-tuple-element.28.refs_1_.refs_3_, f32[32,1024]{1,0:T(8,128)} %copy-done.5, f32[32,1024]{1,0:T(8,128)} %copy-done.4, f32[32,1024]{1,0:T(8,128)} %copy-done.3, ...), custom_call_target="tpu_custom_call" | custom-call | tf_op jit(solution)/shard_map/lora/pallas_call | solution.py:51
  120.3 0.0 collective-permute-done.1.refs_2_.refs_4_
  120.3 0.0 collective-permute-done.6.refs_5_.refs_2_
  120.3 0.0 collective-permute-done.8.refs_7_.refs_3_
  120.3 0.0 all-to-all-done.1
  120.3 10.5 %all-to-all-start.2 = ((bf16[64,8,2560]{2,1,0:T(8,128)(2,1)}), bf16[64,8,2560]{2,1,0:T(8,128)(2,1)}, u32[]{:S(2)}, u32[]{:S(2)}) async-start(bf16[64,8,2560]{2,1,0:T(8,128)(2,1)} %bitcast.17), calls=%async_computation.2 | async-start | bytes 5242880 | tf_op jit(solution)/shard_map/all_to_all | solution.py:312
  130.8 3.2 %weights.2 = (bf16[1280,512]{1,0:T(8,128)(2,1)}, bf16[1280,512]{1,0:T(8,128)(2,1)}) custom-call(s32[1]{0:T(128)} %bitcast.1.refs_0_, bf16[5120,256]{1,0:T(8,128)(2,1)} %refs_1_.9, bf16[5120,256]{1,0:T(8,128)(2,1)} %refs_2_.5, bf16[32,1024]{1,0:T(8,128)(2,1)} %get-tuple-element.29.refs_3_.refs_1_), custom_call_target="tpu_custom_call" | custom-call | tf_op jit(solution)/shard_map/weights/pallas_call | solution.py:51
  134.1 1.1 collective-permute-start.7
  135.2 5.2 %low.1 = (f32[32,1024]{1,0:T(8,128)}, bf16[1024,1280]{1,0:T(8,128)(2,1)}) custom-call(s32[8,1024]{1,0:T(8,128)} %get-tuple-element.27.refs_0_, bf16[512,2560]{1,0:T(8,128)(2,1)} %bitcast.9.refs_1_, bf16[256,1280]{1,0:T(8,128)(2,1)} %bitcast.19, bf16[256,1280]{1,0:T(8,128)(2,1)} %bitcast.21), custom_call_target="tpu_custom_call" | custom-call | tf_op jit(solution)/shard_map/low/pallas_call | solution.py:51
  140.4 1.1 collective-permute-start.11
  141.5 2.9 %collective-permute-start.10 = (f32[32,1024]{1,0:T(8,128)}, f32[32,1024]{1,0:T(8,128)S(1)}, u32[]{:S(2)}, u32[]{:S(2)}) collective-permute-start(f32[32,1024]{1,0:T(8,128)} %get-tuple-element.35.refs_2_), channel_id=1, source_target_pairs={{0,2},{1,3},{2,0},{3,1},{4,6},{5,7},{6,4},{7,5},{8,10},{9,11},{10,... | collective-permute-start | bytes 393224 | tf_op jit(solution)/shard_map/ppermute | solution.py:267
  144.4 0.0 collective-permute-start.9
  144.4 25.3 %collective-permute-done.11.refs_5_ = f32[32,1024]{1,0:T(8,128)S(1)} collective-permute-done((f32[32,1024]{1,0:T(8,128)}, f32[32,1024]{1,0:T(8,128)S(1)}, u32[]{:S(2)}, u32[]{:S(2)}) %collective-permute-start.11) | collective-permute-done | bytes 131104 | tf_op jit(solution)/shard_map/ppermute | solution.py:267
  169.7 0.6 collective-permute-done.10.refs_4_
  170.3 2.0 collective-permute-done.9.refs_3_
  172.3 0.0 copy-done.6
  172.3 0.6 copy-done.8
  173.0 5.1 %grads.1 = (f32[256,1280]{1,0:T(8,128)}, f32[256,1280]{1,0:T(8,128)}, f32[256,256]{1,0:T(8,128)}, f32[256,256]{1,0:T(8,128)}) custom-call(s32[8,1024]{1,0:T(8,128)} %get-tuple-element.27.refs_0_, bf16[32,1024]{1,0:T(8,128)(2,1)} %get-tuple-element.29.refs_3_.refs_1_, f32[32,1024]{1,0:T(8,128)} %get-tuple-element.35.refs_2_, f32[32,1024]{1,0:T(8,128)} %copy-done.8, ...), custom_call_target="tpu_custom_call" | custom-call | tf_op jit(solution)/shard_map/grads/pallas_call | solution.py:51
  178.1 0.0 collective-permute-done.7.refs_6_
  178.1 7.7 %frozen.1.frozen_ref = f32[512,1280]{1,0:T(8,128)} custom-call(bf16[512,512]{1,0:T(8,128)(2,1)} %join.1.refs_0_, bf16[512,512]{1,0:T(8,128)(2,1)} %collective-permute-done.refs_1_, bf16[512,512]{1,0:T(8,128)(2,1)} %collective-permute-done.1.refs_2_.refs_4_, bf16[512,512]{1,0:T(8,128)(2,1)} %copy-done, bf16[1280,512]{1,0:T(8,128)(2,1)} %get-tuple-element.30.refs_4_, ...), custom_call_target="tpu_custom_call" | custom-call | tf_op jit(solution)/shard_map/frozen/pallas_call | solution.py:51
  185.8 7.5 %all-to-all-done.2 = bf16[64,8,2560]{2,1,0:T(8,128)(2,1)} async-done(((bf16[64,8,2560]{2,1,0:T(8,128)(2,1)}), bf16[64,8,2560]{2,1,0:T(8,128)(2,1)}, u32[]{:S(2)}, u32[]{:S(2)}) %all-to-all-start.2) | async-done | bytes 2621472 | tf_op jit(solution)/shard_map/all_to_all | solution.py:312
  193.3 5.0 %final.1 = bf16[512,1280]{1,0:T(8,128)(2,1)} custom-call(bf16[512,1024]{1,0:T(8,128)(2,1)} %get-tuple-element.25.route_ref, f32[512,1280]{1,0:T(8,128)} %frozen.1.frozen_ref, bf16[512,2560]{1,0:T(8,128)(2,1)} %bitcast.11.rows_ref), custom_call_target="tpu_custom_call" | custom-call | tf_op jit(solution)/shard_map/final/pallas_call | solution.py:232
  (13 shorter events, 0.0 us)
Async XLA Ops:
  3.9 43.8 %all-to-all-start = ((bf16[64,8,1152]{2,1,0:T(8,128)(2,1)}), bf16[64,8,1152]{2,1,0:T(8,128)(2,1)}, u32[]{:S(2)}, u32[]{:S(2)}) async-start(bf16[64,8,1152]{2,1,0:T(8,128)(2,1)} %bitcast.22), calls=%async_computation | async-start | bytes 2359296 | tf_op jit(solution)/shard_map/all_to_all | solution.py:292
  18.1 14.6 %collective-permute-start.2 = (bf16[512,512]{1,0:T(8,128)(2,1)}, bf16[512,512]{1,0:T(8,128)(2,1)S(1)}, u32[]{:S(2)}, u32[]{:S(2)}) collective-permute-start(bf16[512,512]{1,0:T(8,128)(2,1)} %join.1.refs_0_), channel_id=1, source_target_pairs={{0,3},{1,0},{2,1},{3,2},{4,7},{5,4},{6,5},{7,6},{8,11},{9,8},{10,9... | collective-permute-start | bytes 1572872 | tf_op jit(solution)/shard_map/ppermute | solution.py:267
  20.9 15.2 %collective-permute-start = (bf16[512,512]{1,0:T(8,128)(2,1)}, bf16[512,512]{1,0:T(8,128)(2,1)}, u32[]{:S(2)}, u32[]{:S(2)}) collective-permute-start(bf16[512,512]{1,0:T(8,128)(2,1)} %join.1.refs_0_), channel_id=1, source_target_pairs={{0,1},{1,2},{2,3},{3,0},{4,5},{5,6},{6,7},{7,4},{8,9},{9,10},{10,1... | collective-permute-start | bytes 1572872 | tf_op jit(solution)/shard_map/ppermute | solution.py:267
  32.7 3.4 %copy-start = (bf16[512,512]{1,0:T(8,128)(2,1)}, bf16[512,512]{1,0:T(8,128)(2,1)S(1)}, u32[]{:S(2)}) copy-start(bf16[512,512]{1,0:T(8,128)(2,1)S(1)} %collective-permute-done.2.refs_2_.refs_3_) | copy-start | bytes 1572868
  47.7 72.6 %all-to-all-start.1 = ((bf16[64,8,2560]{2,1,0:T(8,128)(2,1)}), bf16[64,8,2560]{2,1,0:T(8,128)(2,1)}, u32[]{:S(2)}, u32[]{:S(2)}) async-start(bf16[64,8,2560]{2,1,0:T(8,128)(2,1)} %bitcast.16), calls=%async_computation.1 | async-start | bytes 5242880 | tf_op jit(solution)/shard_map/all_to_all | solution.py:301
  56.4 6.6 %copy-start.1 = (bf16[512,512]{1,0:T(8,128)(2,1)S(1)}, bf16[512,512]{1,0:T(8,128)(2,1)}, u32[]{:S(2)}) copy-start(bf16[512,512]{1,0:T(8,128)(2,1)} %join.1.refs_0_) | copy-start | bytes 1572868
  56.4 8.4 %copy-start.2 = (f32[32,1024]{1,0:T(8,128)S(1)}, f32[32,1024]{1,0:T(8,128)}, u32[]{:S(2)}) copy-start(f32[32,1024]{1,0:T(8,128)} %get-tuple-element.28.refs_1_.refs_3_) | copy-start | bytes 393220
  59.7 60.6 %collective-permute-start.6 = (bf16[1280,512]{1,0:T(8,128)(2,1)}, bf16[1280,512]{1,0:T(8,128)(2,1)}, u32[]{:S(2)}, u32[]{:S(2)}) collective-permute-start(bf16[1280,512]{1,0:T(8,128)(2,1)} %get-tuple-element.31), channel_id=1, source_target_pairs={{0,1},{1,2},{2,3},{3,0},{4,5},{5,6},{6,7},{7,4},{8,9},{9,10},{10,1... | collective-permute-start | bytes 3932168 | tf_op jit(solution)/shard_map/ppermute | solution.py:267
  61.3 59.0 %collective-permute-start.8 = (bf16[1280,512]{1,0:T(8,128)(2,1)}, bf16[1280,512]{1,0:T(8,128)(2,1)}, u32[]{:S(2)}, u32[]{:S(2)}) collective-permute-start(bf16[1280,512]{1,0:T(8,128)(2,1)} %get-tuple-element.33), channel_id=1, source_target_pairs={{0,3},{1,0},{2,1},{3,2},{4,7},{5,4},{6,5},{7,6},{8,11},{9,8},{10,9... | collective-permute-start | bytes 3932168 | tf_op jit(solution)/shard_map/ppermute | solution.py:267
  63.1 57.2 %collective-permute-start.1 = (bf16[512,512]{1,0:T(8,128)(2,1)S(1)}, bf16[512,512]{1,0:T(8,128)(2,1)}, u32[]{:S(2)}, u32[]{:S(2)}) collective-permute-start(bf16[512,512]{1,0:T(8,128)(2,1)S(1)} %copy-done.1), channel_id=1, source_target_pairs={{0,2},{1,3},{2,0},{3,1},{4,6},{5,7},{6,4},{7,5},{8,10},{9,11},{10,... | collective-permute-start | bytes 1572872 | tf_op jit(solution)/shard_map/ppermute | solution.py:267
  64.9 43.3 %collective-permute-start.5 = (f32[32,1024]{1,0:T(8,128)S(1)}, f32[32,1024]{1,0:T(8,128)S(1)}, u32[]{:S(2)}, u32[]{:S(2)}) collective-permute-start(f32[32,1024]{1,0:T(8,128)S(1)} %copy-done.2), channel_id=1, source_target_pairs={{0,3},{1,0},{2,1},{3,2},{4,7},{5,4},{6,5},{7,6},{8,11},{9,8},{10,9... | collective-permute-start | bytes 393224 | tf_op jit(solution)/shard_map/ppermute | solution.py:267
  66.0 42.2 %collective-permute-start.4 = (f32[32,1024]{1,0:T(8,128)S(1)}, f32[32,1024]{1,0:T(8,128)S(1)}, u32[]{:S(2)}, u32[]{:S(2)}) collective-permute-start(f32[32,1024]{1,0:T(8,128)S(1)} %copy-done.2), channel_id=1, source_target_pairs={{0,2},{1,3},{2,0},{3,1},{4,6},{5,7},{6,4},{7,5},{8,10},{9,11},{10,... | collective-permute-start | bytes 393224 | tf_op jit(solution)/shard_map/ppermute | solution.py:267
  108.2 7.3 %copy-start.3 = (f32[32,1024]{1,0:T(8,128)}, f32[32,1024]{1,0:T(8,128)S(1)}, u32[]{:S(2)}) copy-start(f32[32,1024]{1,0:T(8,128)S(1)} %collective-permute-done.5.refs_4_) | copy-start | bytes 393220
  108.2 6.6 %collective-permute-start.3 = (f32[32,1024]{1,0:T(8,128)S(1)}, f32[32,1024]{1,0:T(8,128)S(1)}, u32[]{:S(2)}, u32[]{:S(2)}) collective-permute-start(f32[32,1024]{1,0:T(8,128)S(1)} %copy-done.2), channel_id=1, source_target_pairs={{0,1},{1,2},{2,3},{3,0},{4,5},{5,6},{6,7},{7,4},{8,9},{9,10},{10,1... | collective-permute-start | bytes 393224 | tf_op jit(solution)/shard_map/ppermute | solution.py:267
  108.2 7.3 %copy-start.4 = (f32[32,1024]{1,0:T(8,128)}, f32[32,1024]{1,0:T(8,128)S(1)}, u32[]{:S(2)}) copy-start(f32[32,1024]{1,0:T(8,128)S(1)} %collective-permute-done.4.refs_3_) | copy-start | bytes 393220
  114.8 0.7 copy-start.5
  120.3 72.9 %all-to-all-start.2 = ((bf16[64,8,2560]{2,1,0:T(8,128)(2,1)}), bf16[64,8,2560]{2,1,0:T(8,128)(2,1)}, u32[]{:S(2)}, u32[]{:S(2)}) async-start(bf16[64,8,2560]{2,1,0:T(8,128)(2,1)} %bitcast.17), calls=%async_computation.2 | async-start | bytes 5242880 | tf_op jit(solution)/shard_map/all_to_all | solution.py:312
  134.1 44.0 %collective-permute-start.7 = (bf16[1280,512]{1,0:T(8,128)(2,1)}, bf16[1280,512]{1,0:T(8,128)(2,1)}, u32[]{:S(2)}, u32[]{:S(2)}) collective-permute-start(bf16[1280,512]{1,0:T(8,128)(2,1)} %get-tuple-element.32), channel_id=1, source_target_pairs={{0,2},{1,3},{2,0},{3,1},{4,6},{5,7},{6,4},{7,5},{8,10},{9,11},{10,... | collective-permute-start | bytes 3932168 | tf_op jit(solution)/shard_map/ppermute | solution.py:267
  140.4 29.3 %collective-permute-start.11 = (f32[32,1024]{1,0:T(8,128)}, f32[32,1024]{1,0:T(8,128)S(1)}, u32[]{:S(2)}, u32[]{:S(2)}) collective-permute-start(f32[32,1024]{1,0:T(8,128)} %get-tuple-element.35.refs_2_), channel_id=1, source_target_pairs={{0,3},{1,0},{2,1},{3,2},{4,7},{5,4},{6,5},{7,6},{8,11},{9,8},{10,9... | collective-permute-start | bytes 393224 | tf_op jit(solution)/shard_map/ppermute | solution.py:267
  141.5 28.8 %collective-permute-start.10 = (f32[32,1024]{1,0:T(8,128)}, f32[32,1024]{1,0:T(8,128)S(1)}, u32[]{:S(2)}, u32[]{:S(2)}) collective-permute-start(f32[32,1024]{1,0:T(8,128)} %get-tuple-element.35.refs_2_), channel_id=1, source_target_pairs={{0,2},{1,3},{2,0},{3,1},{4,6},{5,7},{6,4},{7,5},{8,10},{9,11},{10,... | collective-permute-start | bytes 393224 | tf_op jit(solution)/shard_map/ppermute | solution.py:267
  144.4 27.9 %collective-permute-start.9 = (f32[32,1024]{1,0:T(8,128)}, f32[32,1024]{1,0:T(8,128)S(1)}, u32[]{:S(2)}, u32[]{:S(2)}) collective-permute-start(f32[32,1024]{1,0:T(8,128)} %get-tuple-element.35.refs_2_), channel_id=1, source_target_pairs={{0,1},{1,2},{2,3},{3,0},{4,5},{5,6},{6,7},{7,4},{8,9},{9,10},{10,1... | collective-permute-start | bytes 393224 | tf_op jit(solution)/shard_map/ppermute | solution.py:267
  169.7 2.6 %copy-start.6 = (f32[32,1024]{1,0:T(8,128)}, f32[32,1024]{1,0:T(8,128)S(1)}, u32[]{:S(2)}) copy-start(f32[32,1024]{1,0:T(8,128)S(1)} %collective-permute-done.11.refs_5_) | copy-start | bytes 393220
  170.3 2.0 copy-start.7
  172.3 0.6 copy-start.8

commit v4 on v3

--- a/solution.py
+++ b/solution.py
@@ -297,7 +297,7 @@
         grad_key, grad_value
     )
     every = [both] + [shift_tensor(both, s) for s in (1, 2, 3)]
-    placed = hold(placed, [every[1], every[3]])
+    placed = hold(placed, every[1:])
     held = lax.all_to_all(placed, "adapter", split_axis=0, concat_axis=0, tiled=True)
     part, code, got = call(
         back_kernel,
@@ -308,7 +308,7 @@
     rows, back = call(
         lora_kernel, [((slots // 2, 2 * width), bf16), ((2 * rank, slots), bf16)], "lora"
     )(code, *sums, down_key, down_value)
-    rows = hold(rows, [held, blocks[1], blocks[3], every[2]])
+    rows = hold(rows, [held, blocks[1], blocks[3]])
     returned = lax.all_to_all(rows, "adapter", split_axis=0, concat_axis=0, tiled=True)
     blocks |= weights((0, 2), [back])
     part, held = call(

time: 199 us -> 194 us (0.975)
  waiting for transfers between devices: 105 us -> 101 us
    all_to_all x1, waiting for transfers between devices: 0.01 us -> 12.9 us  [local(): lax.all_to_all(placed, 'adapter', split_axis=0, concat_axis=0, tiled=True)]
    all_to_all x1, waiting for transfers between devices: 11.6 us -> 0.04 us  [local(): lax.all_to_all(sent, 'adapter', split_axis=0, concat_axis=0, tiled=True)]
    all_to_all x1, starting transfers between devices: 10.5 us -> 5.6 us  [local(): lax.all_to_all(rows, 'adapter', split_axis=0, concat_axis=0, tiled=True)]
    ppermute x12, waiting for transfers between devices: 85.6 us -> 80.8 us  [shift_tensor(): return lax.ppermute(x, 'tensor', [(i, (i + s) % 4) for i in range(4)])]
    all_to_all x1, starting transfers between devices: 5.79 us -> 10.4 us  [local(): lax.all_to_all(placed, 'adapter', split_axis=0, concat_axis=0, tiled=True)]
where the time goes in v4:
time: 194 us
  waiting for transfers between devices  101 us (52%)
  Pallas kernels  47.1 us (24%)
  starting transfers between devices  43.3 us (22%)
    ppermute x12, waiting for transfers between devices, shift_tensor(): return lax.ppermute(x, 'tensor', [(i, (i + s) % 4) for i in range(4)])  80.8 us
    pallas_call x10, Pallas kernels, run(): pl.pallas_call(body, out_shape=[jax.ShapeDtypeStruct(s, d) for s, d in ou...  42.1 us
    ppermute x12, starting transfers between devices, shift_tensor(): return lax.ppermute(x, 'tensor', [(i, (i + s) % 4) for i in range(4)])  15 us
    all_to_all x1, waiting for transfers between devices, local(): lax.all_to_all(placed, 'adapter', split_axis=0, concat_axis=0, tiled=True)  12.9 us
    all_to_all x1, starting transfers between devices, local(): lax.all_to_all(sent, 'adapter', split_axis=0, concat_axis=0, tiled=True)  12.3 us
    all_to_all x1, starting transfers between devices, local(): lax.all_to_all(placed, 'adapter', split_axis=0, concat_axis=0, tiled=True)  10.4 us
    all_to_all x1, waiting for transfers between devices, local(): lax.all_to_all(rows, 'adapter', split_axis=0, concat_axis=0, tiled=True)  7.49 us
    all_to_all x1, starting transfers between devices, local(): lax.all_to_all(rows, 'adapter', split_axis=0, concat_axis=0, tiled=True)  5.6 us
  transfers between devices with their start and end apart: 15, of which 9 were waited for; matrix products, arithmetic and copies ran while one was open for 0% of the time, Pallas kernels for 20%

profile of v4, /device:TPU:8, one launch (start us, length us, event | category | flops | bytes accessed | tf_op | source)
XLA Modules:
  0.0 193.8 jit_solution(16513734515807572604)
XLA Ops:
  0.6 3.2 %route.1 = (s32[8,512]{1,0:T(8,128)}, bf16[512,1152]{1,0:T(8,128)(2,1)}) custom-call(s32[1,512]{1,0:T(1,128)} %bitcast.26, bf16[512,256]{1,0:T(8,128)(2,1)} %refs_0_.1, bf16[512,256]{1,0:T(8,128)(2,1)} %refs_1_.7), custom_call_target="tpu_custom_call" | custom-call | tf_op jit(solution)/shard_map/route/pallas_call | solution.py:51
  3.9 12.3 %all-to-all-start = ((bf16[64,8,1152]{2,1,0:T(8,128)(2,1)}), bf16[64,8,1152]{2,1,0:T(8,128)(2,1)}, u32[]{:S(2)}, u32[]{:S(2)}) async-start(bf16[64,8,1152]{2,1,0:T(8,128)(2,1)} %bitcast.22), calls=%async_computation | async-start | bytes 2359296 | tf_op jit(solution)/shard_map/all_to_all | solution.py:292
  16.2 1.9 join.1.refs_0_
  18.1 2.8 %collective-permute-start.2 = (bf16[512,512]{1,0:T(8,128)(2,1)}, bf16[512,512]{1,0:T(8,128)(2,1)S(1)}, u32[]{:S(2)}, u32[]{:S(2)}) collective-permute-start(bf16[512,512]{1,0:T(8,128)(2,1)} %join.1.refs_0_), channel_id=1, source_target_pairs={{0,3},{1,0},{2,1},{3,2},{4,7},{5,4},{6,5},{7,6},{8,11},{9,8},{10,9... | collective-permute-start | bytes 1572872 | tf_op jit(solution)/shard_map/ppermute | solution.py:267
  20.9 0.8 collective-permute-start.1
  21.7 0.9 collective-permute-start
  22.6 4.8 %place.1 = (bf16[512,2560]{1,0:T(8,128)(2,1)}, bf16[512,1024]{1,0:T(8,128)(2,1)}) custom-call(s32[8,512]{1,0:T(8,128)} %get-tuple-element.24.refs_0_.refs_2_, bf16[512,1280]{1,0:T(8,128)(2,1)} %refs_1_.6), custom_call_target="tpu_custom_call" | custom-call | tf_op jit(solution)/shard_map/place/pallas_call | solution.py:51
  27.4 16.6 %collective-permute-done.2.refs_3_ = bf16[512,512]{1,0:T(8,128)(2,1)S(1)} collective-permute-done((bf16[512,512]{1,0:T(8,128)(2,1)}, bf16[512,512]{1,0:T(8,128)(2,1)S(1)}, u32[]{:S(2)}, u32[]{:S(2)}) %collective-permute-start.2) | collective-permute-done | bytes 524320 | tf_op jit(solution)/shard_map/ppermute | solution.py:267
  44.0 0.0 collective-permute-done.1.refs_2_
  44.0 3.7 %collective-permute-done.refs_1_ = bf16[512,512]{1,0:T(8,128)(2,1)} collective-permute-done((bf16[512,512]{1,0:T(8,128)(2,1)}, bf16[512,512]{1,0:T(8,128)(2,1)}, u32[]{:S(2)}, u32[]{:S(2)}) %collective-permute-start) | collective-permute-done | bytes 524320 | tf_op jit(solution)/shard_map/ppermute | solution.py:267
  47.7 0.0 copy-done
  47.7 0.0 all-to-all-done
  47.7 10.4 %all-to-all-start.1 = ((bf16[64,8,2560]{2,1,0:T(8,128)(2,1)}), bf16[64,8,2560]{2,1,0:T(8,128)(2,1)}, u32[]{:S(2)}, u32[]{:S(2)}) async-start(bf16[64,8,2560]{2,1,0:T(8,128)(2,1)} %bitcast.17), calls=%async_computation.1 | async-start | bytes 5242880 | tf_op jit(solution)/shard_map/all_to_all | solution.py:301
  58.1 2.9 %back.1 = (f32[32,1024]{1,0:T(8,128)}, s32[8,1024]{1,0:T(8,128)}, bf16[1024,512]{1,0:T(8,128)(2,1)}) custom-call(bf16[512,1152]{1,0:T(8,128)(2,1)} %bitcast.3.refs_0_, bf16[256,256]{1,0:T(8,128)(2,1)} %bitcast.24, bf16[256,256]{1,0:T(8,128)(2,1)} %bitcast.25), custom_call_target="tpu_custom_call" | custom-call | tf_op jit(solution)/shard_map/back/pallas_call | solution.py:51
  61.1 0.0 copy-start.1
  61.1 3.3 %weights.3 = (bf16[1280,512]{1,0:T(8,128)(2,1)}, bf16[1280,512]{1,0:T(8,128)(2,1)}) custom-call(s32[1]{0:T(128)} %bitcast.1.refs_0_, bf16[5120,256]{1,0:T(8,128)(2,1)} %refs_1_.9, bf16[5120,256]{1,0:T(8,128)(2,1)} %refs_2_.5, f32[32,1024]{1,0:T(8,128)} %get-tuple-element.28.refs_1_.refs_3_), custom_call_target="tpu_custom_call" | custom-call | tf_op jit(solution)/shard_map/weights/pallas_call | solution.py:51
  64.3 0.1 collective-permute-start.6
  64.4 3.2 %collective-permute-start.8 = (bf16[1280,512]{1,0:T(8,128)(2,1)}, bf16[1280,512]{1,0:T(8,128)(2,1)}, u32[]{:S(2)}, u32[]{:S(2)}) collective-permute-start(bf16[1280,512]{1,0:T(8,128)(2,1)} %get-tuple-element.33), channel_id=1, source_target_pairs={{0,3},{1,0},{2,1},{3,2},{4,7},{5,4},{6,5},{7,6},{8,11},{9,8},{10,9... | collective-permute-start | bytes 3932168 | tf_op jit(solution)/shard_map/ppermute | solution.py:267
  67.6 0.0 copy-done.1
  67.6 0.0 collective-permute-start.5
  67.7 0.9 collective-permute-start.4
  68.6 1.1 collective-permute-start.3
  69.7 31.9 %collective-permute-done.5.refs_4_ = f32[32,1024]{1,0:T(8,128)S(1)} collective-permute-done((f32[32,1024]{1,0:T(8,128)S(1)}, f32[32,1024]{1,0:T(8,128)S(1)}, u32[]{:S(2)}, u32[]{:S(2)}) %collective-permute-start.5) | collective-permute-done | bytes 131104 | tf_op jit(solution)/shard_map/ppermute | solution.py:267
  101.5 0.0 collective-permute-done.4.refs_3_
  101.6 0.7 collective-permute-done.3.refs_2_
  102.3 0.0 copy-done.3
  102.3 0.6 copy-done.4
  102.9 4.8 %lora.1 = (bf16[512,2560]{1,0:T(8,128)(2,1)}, bf16[32,1024]{1,0:T(8,128)(2,1)}) custom-call(s32[8,1024]{1,0:T(8,128)} %get-tuple-element.27.refs_0_, f32[32,1024]{1,0:T(8,128)} %get-tuple-element.28.refs_1_.refs_3_, f32[32,1024]{1,0:T(8,128)} %copy-done.4, f32[32,1024]{1,0:T(8,128)} %copy-done.3, f32[32,1024]{1,0:T(8,128)} %copy-done.2, ...), custom_call_target="tpu_custom_call" | custom-call | tf_op jit(solution)/shard_map/lora/pallas_call | solution.py:51
  107.7 0.0 collective-permute-done.6.refs_5_.refs_2_
  107.7 0.0 collective-permute-done.8.refs_7_.refs_3_
  107.7 12.9 %all-to-all-done.1 = bf16[64,8,2560]{2,1,0:T(8,128)(2,1)} async-done(((bf16[64,8,2560]{2,1,0:T(8,128)(2,1)}), bf16[64,8,2560]{2,1,0:T(8,128)(2,1)}, u32[]{:S(2)}, u32[]{:S(2)}) %all-to-all-start.1) | async-done | bytes 2621472 | tf_op jit(solution)/shard_map/all_to_all | solution.py:301
  120.6 5.6 %all-to-all-start.2 = ((bf16[64,8,2560]{2,1,0:T(8,128)(2,1)}), bf16[64,8,2560]{2,1,0:T(8,128)(2,1)}, u32[]{:S(2)}, u32[]{:S(2)}) async-start(bf16[64,8,2560]{2,1,0:T(8,128)(2,1)} %bitcast.16), calls=%async_computation.2 | async-start | bytes 5242880 | tf_op jit(solution)/shard_map/all_to_all | solution.py:312
  126.2 3.3 %weights.2 = (bf16[1280,512]{1,0:T(8,128)(2,1)}, bf16[1280,512]{1,0:T(8,128)(2,1)}) custom-call(s32[1]{0:T(128)} %bitcast.1.refs_0_, bf16[5120,256]{1,0:T(8,128)(2,1)} %refs_1_.9, bf16[5120,256]{1,0:T(8,128)(2,1)} %refs_2_.5, bf16[32,1024]{1,0:T(8,128)(2,1)} %get-tuple-element.29.refs_3_.refs_1_), custom_call_target="tpu_custom_call" | custom-call | tf_op jit(solution)/shard_map/weights/pallas_call | solution.py:51
  129.4 0.9 collective-permute-start.7
  130.3 5.2 %low.1 = (f32[32,1024]{1,0:T(8,128)}, bf16[1024,1280]{1,0:T(8,128)(2,1)}) custom-call(s32[8,1024]{1,0:T(8,128)} %get-tuple-element.27.refs_0_, bf16[512,2560]{1,0:T(8,128)(2,1)} %bitcast.9.refs_1_, bf16[256,1280]{1,0:T(8,128)(2,1)} %bitcast.19, bf16[256,1280]{1,0:T(8,128)(2,1)} %bitcast.21), custom_call_target="tpu_custom_call" | custom-call | tf_op jit(solution)/shard_map/low/pallas_call | solution.py:51
  135.6 1.3 collective-permute-start.11
  136.9 1.6 collective-permute-start.10
  138.5 1.3 collective-permute-start.9
  139.8 23.9 %collective-permute-done.11.refs_5_ = f32[32,1024]{1,0:T(8,128)S(1)} collective-permute-done((f32[32,1024]{1,0:T(8,128)}, f32[32,1024]{1,0:T(8,128)S(1)}, u32[]{:S(2)}, u32[]{:S(2)}) %collective-permute-start.11) | collective-permute-done | bytes 131104 | tf_op jit(solution)/shard_map/ppermute | solution.py:267
  163.7 2.0 %collective-permute-done.10.refs_4_ = f32[32,1024]{1,0:T(8,128)S(1)} collective-permute-done((f32[32,1024]{1,0:T(8,128)}, f32[32,1024]{1,0:T(8,128)S(1)}, u32[]{:S(2)}, u32[]{:S(2)}) %collective-permute-start.10) | collective-permute-done | bytes 131104 | tf_op jit(solution)/shard_map/ppermute | solution.py:267
  165.7 2.0 %collective-permute-done.9.refs_3_ = f32[32,1024]{1,0:T(8,128)S(1)} collective-permute-done((f32[32,1024]{1,0:T(8,128)}, f32[32,1024]{1,0:T(8,128)S(1)}, u32[]{:S(2)}, u32[]{:S(2)}) %collective-permute-start.9) | collective-permute-done | bytes 131104 | tf_op jit(solution)/shard_map/ppermute | solution.py:267
  167.7 0.0 copy-done.6
  167.7 0.6 copy-done.7
  168.3 5.1 %grads.1 = (f32[256,1280]{1,0:T(8,128)}, f32[256,1280]{1,0:T(8,128)}, f32[256,256]{1,0:T(8,128)}, f32[256,256]{1,0:T(8,128)}) custom-call(s32[8,1024]{1,0:T(8,128)} %get-tuple-element.27.refs_0_, bf16[32,1024]{1,0:T(8,128)(2,1)} %get-tuple-element.29.refs_3_.refs_1_, f32[32,1024]{1,0:T(8,128)} %get-tuple-element.35.refs_2_, f32[32,1024]{1,0:T(8,128)} %copy-done.7, ...), custom_call_target="tpu_custom_call" | custom-call | tf_op jit(solution)/shard_map/grads/pallas_call | solution.py:51
  173.5 0.0 collective-permute-done.7.refs_6_
  173.5 7.7 %frozen.1.frozen_ref = f32[512,1280]{1,0:T(8,128)} custom-call(bf16[512,512]{1,0:T(8,128)(2,1)} %join.1.refs_0_, bf16[512,512]{1,0:T(8,128)(2,1)} %collective-permute-done.refs_1_, bf16[512,512]{1,0:T(8,128)(2,1)} %collective-permute-done.1.refs_2_, bf16[512,512]{1,0:T(8,128)(2,1)} %copy-done, bf16[1280,512]{1,0:T(8,128)(2,1)} %get-tuple-element.30.refs_4_, ...), custom_call_target="tpu_custom_call" | custom-call | tf_op jit(solution)/shard_map/frozen/pallas_call | solution.py:51
  181.2 7.5 %all-to-all-done.2 = bf16[64,8,2560]{2,1,0:T(8,128)(2,1)} async-done(((bf16[64,8,2560]{2,1,0:T(8,128)(2,1)}), bf16[64,8,2560]{2,1,0:T(8,128)(2,1)}, u32[]{:S(2)}, u32[]{:S(2)}) %all-to-all-start.2) | async-done | bytes 2621472 | tf_op jit(solution)/shard_map/all_to_all | solution.py:312
  188.7 5.0 %final.1 = bf16[512,1280]{1,0:T(8,128)(2,1)} custom-call(bf16[512,1024]{1,0:T(8,128)(2,1)} %get-tuple-element.25.route_ref, f32[512,1280]{1,0:T(8,128)} %frozen.1.frozen_ref, bf16[512,2560]{1,0:T(8,128)(2,1)} %bitcast.11.rows_ref), custom_call_target="tpu_custom_call" | custom-call | tf_op jit(solution)/shard_map/final/pallas_call | solution.py:232
  (11 shorter events, 0.0 us)
Async XLA Ops:
  3.9 43.8 %all-to-all-start = ((bf16[64,8,1152]{2,1,0:T(8,128)(2,1)}), bf16[64,8,1152]{2,1,0:T(8,128)(2,1)}, u32[]{:S(2)}, u32[]{:S(2)}) async-start(bf16[64,8,1152]{2,1,0:T(8,128)(2,1)} %bitcast.22), calls=%async_computation | async-start | bytes 2359296 | tf_op jit(solution)/shard_map/all_to_all | solution.py:292
  18.1 25.9 %collective-permute-start.2 = (bf16[512,512]{1,0:T(8,128)(2,1)}, bf16[512,512]{1,0:T(8,128)(2,1)S(1)}, u32[]{:S(2)}, u32[]{:S(2)}) collective-permute-start(bf16[512,512]{1,0:T(8,128)(2,1)} %join.1.refs_0_), channel_id=1, source_target_pairs={{0,3},{1,0},{2,1},{3,2},{4,7},{5,4},{6,5},{7,6},{8,11},{9,8},{10,9... | collective-permute-start | bytes 1572872 | tf_op jit(solution)/shard_map/ppermute | solution.py:267
  20.9 23.1 %collective-permute-start.1 = (bf16[512,512]{1,0:T(8,128)(2,1)}, bf16[512,512]{1,0:T(8,128)(2,1)}, u32[]{:S(2)}, u32[]{:S(2)}) collective-permute-start(bf16[512,512]{1,0:T(8,128)(2,1)} %join.1.refs_0_), channel_id=1, source_target_pairs={{0,2},{1,3},{2,0},{3,1},{4,6},{5,7},{6,4},{7,5},{8,10},{9,11},{10,... | collective-permute-start | bytes 1572872 | tf_op jit(solution)/shard_map/ppermute | solution.py:267
  21.7 26.0 %collective-permute-start = (bf16[512,512]{1,0:T(8,128)(2,1)}, bf16[512,512]{1,0:T(8,128)(2,1)}, u32[]{:S(2)}, u32[]{:S(2)}) collective-permute-start(bf16[512,512]{1,0:T(8,128)(2,1)} %join.1.refs_0_), channel_id=1, source_target_pairs={{0,1},{1,2},{2,3},{3,0},{4,5},{5,6},{6,7},{7,4},{8,9},{9,10},{10,1... | collective-permute-start | bytes 1572872 | tf_op jit(solution)/shard_map/ppermute | solution.py:267
  44.0 3.7 %copy-start = (bf16[512,512]{1,0:T(8,128)(2,1)}, bf16[512,512]{1,0:T(8,128)(2,1)S(1)}, u32[]{:S(2)}) copy-start(bf16[512,512]{1,0:T(8,128)(2,1)S(1)} %collective-permute-done.2.refs_3_) | copy-start | bytes 1572868
  47.7 72.9 %all-to-all-start.1 = ((bf16[64,8,2560]{2,1,0:T(8,128)(2,1)}), bf16[64,8,2560]{2,1,0:T(8,128)(2,1)}, u32[]{:S(2)}, u32[]{:S(2)}) async-start(bf16[64,8,2560]{2,1,0:T(8,128)(2,1)} %bitcast.17), calls=%async_computation.1 | async-start | bytes 5242880 | tf_op jit(solution)/shard_map/all_to_all | solution.py:301
  61.1 6.6 %copy-start.1 = (f32[32,1024]{1,0:T(8,128)S(1)}, f32[32,1024]{1,0:T(8,128)}, u32[]{:S(2)}) copy-start(f32[32,1024]{1,0:T(8,128)} %get-tuple-element.28.refs_1_.refs_3_) | copy-start | bytes 393220
  64.3 43.4 %collective-permute-start.6 = (bf16[1280,512]{1,0:T(8,128)(2,1)}, bf16[1280,512]{1,0:T(8,128)(2,1)}, u32[]{:S(2)}, u32[]{:S(2)}) collective-permute-start(bf16[1280,512]{1,0:T(8,128)(2,1)} %get-tuple-element.31), channel_id=1, source_target_pairs={{0,1},{1,2},{2,3},{3,0},{4,5},{5,6},{6,7},{7,4},{8,9},{9,10},{10,1... | collective-permute-start | bytes 3932168 | tf_op jit(solution)/shard_map/ppermute | solution.py:267
  64.4 43.3 %collective-permute-start.8 = (bf16[1280,512]{1,0:T(8,128)(2,1)}, bf16[1280,512]{1,0:T(8,128)(2,1)}, u32[]{:S(2)}, u32[]{:S(2)}) collective-permute-start(bf16[1280,512]{1,0:T(8,128)(2,1)} %get-tuple-element.33), channel_id=1, source_target_pairs={{0,3},{1,0},{2,1},{3,2},{4,7},{5,4},{6,5},{7,6},{8,11},{9,8},{10,9... | collective-permute-start | bytes 3932168 | tf_op jit(solution)/shard_map/ppermute | solution.py:267
  67.6 33.9 %collective-permute-start.5 = (f32[32,1024]{1,0:T(8,128)S(1)}, f32[32,1024]{1,0:T(8,128)S(1)}, u32[]{:S(2)}, u32[]{:S(2)}) collective-permute-start(f32[32,1024]{1,0:T(8,128)S(1)} %copy-done.1), channel_id=1, source_target_pairs={{0,3},{1,0},{2,1},{3,2},{4,7},{5,4},{6,5},{7,6},{8,11},{9,8},{10,9... | collective-permute-start | bytes 393224 | tf_op jit(solution)/shard_map/ppermute | solution.py:267
  67.7 33.9 %collective-permute-start.4 = (f32[32,1024]{1,0:T(8,128)S(1)}, f32[32,1024]{1,0:T(8,128)S(1)}, u32[]{:S(2)}, u32[]{:S(2)}) collective-permute-start(f32[32,1024]{1,0:T(8,128)S(1)} %copy-done.1), channel_id=1, source_target_pairs={{0,2},{1,3},{2,0},{3,1},{4,6},{5,7},{6,4},{7,5},{8,10},{9,11},{10,... | collective-permute-start | bytes 393224 | tf_op jit(solution)/shard_map/ppermute | solution.py:267
  68.6 33.7 %collective-permute-start.3 = (f32[32,1024]{1,0:T(8,128)S(1)}, f32[32,1024]{1,0:T(8,128)S(1)}, u32[]{:S(2)}, u32[]{:S(2)}) collective-permute-start(f32[32,1024]{1,0:T(8,128)S(1)} %copy-done.1), channel_id=1, source_target_pairs={{0,1},{1,2},{2,3},{3,0},{4,5},{5,6},{6,7},{7,4},{8,9},{9,10},{10,1... | collective-permute-start | bytes 393224 | tf_op jit(solution)/shard_map/ppermute | solution.py:267
  101.5 0.7 copy-start.2
  101.5 0.7 copy-start.3
  102.3 0.7 copy-start.4
  120.6 68.1 %all-to-all-start.2 = ((bf16[64,8,2560]{2,1,0:T(8,128)(2,1)}), bf16[64,8,2560]{2,1,0:T(8,128)(2,1)}, u32[]{:S(2)}, u32[]{:S(2)}) async-start(bf16[64,8,2560]{2,1,0:T(8,128)(2,1)} %bitcast.16), calls=%async_computation.2 | async-start | bytes 5242880 | tf_op jit(solution)/shard_map/all_to_all | solution.py:312
  129.4 44.0 %collective-permute-start.7 = (bf16[1280,512]{1,0:T(8,128)(2,1)}, bf16[1280,512]{1,0:T(8,128)(2,1)}, u32[]{:S(2)}, u32[]{:S(2)}) collective-permute-start(bf16[1280,512]{1,0:T(8,128)(2,1)} %get-tuple-element.32), channel_id=1, source_target_pairs={{0,2},{1,3},{2,0},{3,1},{4,6},{5,7},{6,4},{7,5},{8,10},{9,11},{10,... | collective-permute-start | bytes 3932168 | tf_op jit(solution)/shard_map/ppermute | solution.py:267
  135.6 28.1 %collective-permute-start.11 = (f32[32,1024]{1,0:T(8,128)}, f32[32,1024]{1,0:T(8,128)S(1)}, u32[]{:S(2)}, u32[]{:S(2)}) collective-permute-start(f32[32,1024]{1,0:T(8,128)} %get-tuple-element.35.refs_2_), channel_id=1, source_target_pairs={{0,3},{1,0},{2,1},{3,2},{4,7},{5,4},{6,5},{7,6},{8,11},{9,8},{10,9... | collective-permute-start | bytes 393224 | tf_op jit(solution)/shard_map/ppermute | solution.py:267
  136.9 28.9 %collective-permute-start.10 = (f32[32,1024]{1,0:T(8,128)}, f32[32,1024]{1,0:T(8,128)S(1)}, u32[]{:S(2)}, u32[]{:S(2)}) collective-permute-start(f32[32,1024]{1,0:T(8,128)} %get-tuple-element.35.refs_2_), channel_id=1, source_target_pairs={{0,2},{1,3},{2,0},{3,1},{4,6},{5,7},{6,4},{7,5},{8,10},{9,11},{10,... | collective-permute-start | bytes 393224 | tf_op jit(solution)/shard_map/ppermute | solution.py:267
  138.5 29.2 %collective-permute-start.9 = (f32[32,1024]{1,0:T(8,128)}, f32[32,1024]{1,0:T(8,128)S(1)}, u32[]{:S(2)}, u32[]{:S(2)}) collective-permute-start(f32[32,1024]{1,0:T(8,128)} %get-tuple-element.35.refs_2_), channel_id=1, source_target_pairs={{0,1},{1,2},{2,3},{3,0},{4,5},{5,6},{6,7},{7,4},{8,9},{9,10},{10,1... | collective-permute-start | bytes 393224 | tf_op jit(solution)/shard_map/ppermute | solution.py:267
  163.7 4.0 %copy-start.5 = (f32[32,1024]{1,0:T(8,128)}, f32[32,1024]{1,0:T(8,128)S(1)}, u32[]{:S(2)}) copy-start(f32[32,1024]{1,0:T(8,128)S(1)} %collective-permute-done.11.refs_5_) | copy-start | bytes 393220
  165.7 2.0 %copy-start.6 = (f32[32,1024]{1,0:T(8,128)}, f32[32,1024]{1,0:T(8,128)S(1)}, u32[]{:S(2)}) copy-start(f32[32,1024]{1,0:T(8,128)S(1)} %collective-permute-done.10.refs_4_) | copy-start | bytes 393220
  167.7 0.6 copy-start.7
